TPU v7x, 32 devices: a whole 2x2x4 slice. The times are simulated.
32 devices in a mesh: role: 2 (over x), batch: 16 (over z, y, core).
Axes of the slice: x: 2, y: 2, z: 4, core: 2. Of those that a mesh axis runs over, the one named last changes fastest.
Arguments:
- frames: float32 [2, 3584, 4, 7056], P('role', 'batch'), may hold values from 0 to 1
- conv1_weight: bfloat16 [2, 256, 32], P('role'), may hold values from -0.375 to 0.375
- conv1_bias: float32 [2, 32], P('role'), may hold values from -1.5 to 1.5
- conv2_weight: bfloat16 [2, 512, 64], P('role'), may hold values from -0.25 to 0.25
- conv2_bias: float32 [2, 64], P('role'), may hold values from -1.5 to 1.5
- conv3_weight: bfloat16 [2, 576, 64], P('role'), may hold values from -0.25 to 0.25
- conv3_bias: float32 [2, 64], P('role'), may hold values from -1.5 to 1.5
- dense_weight: bfloat16 [2, 3136, 512], P('role'), may hold values from -0.109375 to 0.109375
- dense_bias: float32 [2, 512], P('role'), may hold values from -1.5 to 1.5
- head_weight: bfloat16 [2, 512, 918], P('role'), may hold values from -0.5 to 0.5
- head_bias: float32 [2, 918], P('role'), may hold values from -2.5 to 2.5
- taken_actions: int32 [3584], P('batch'), may hold values from 0 to 17
- next_actions: int32 [3584], P('batch'), may hold values from 0 to 17
- rewards: float32 [3584], P('batch'), may hold values from -12 to 12
- discounts: float32 [3584], P('batch'), may hold values from 0 to 0.99
- importance: float32 [3584], P('batch'), may hold values from 0.1 to 3, as said below
- buffer_slots: int32 [3584], P('batch'), may hold values from 0 to 3583, each once
Outputs:
- frame_grad: float32 [3584, 4, 7056], P('batch', 'role')
- conv1_weight_grad: float32 [256, 32], replicated
- conv1_bias_grad: float32 [32], replicated
- conv2_weight_grad: float32 [512, 64], replicated
- conv2_bias_grad: float32 [64], replicated
- conv3_weight_grad: float32 [576, 64], replicated
- conv3_bias_grad: float32 [64], replicated
- dense_weight_grad: float32 [3136, 512], replicated
- dense_bias_grad: float32 [512], replicated
- head_weight_grad: float32 [512, 918], replicated
- head_bias_grad: float32 [918], replicated
- priorities: float32 [3584], P(('role', 'batch'))
Inputs may be any that keep to these rules, and one draw needn't show every extreme that they name: importance weights are positive.
All inputs are finite; a program needn't handle non-finite values.
Results may differ from a plain program's by a relative error of at most 0.0085.
Values may be sent and summed in bfloat16 or wider, within the bound.
A program may use at most 192 MiB of HBM per device.

v0:
```python
import jax
import jax.numpy as jnp
from jax import lax
from jax.sharding import PartitionSpec as P

STACK = 4
SIDE = 84
ACTIONS = 18
ATOMS = 51


def shifted_2(array, axis, by):
    devices = lax.axis_size(axis)
    pairs = [(i, i + by) for i in range(devices) if 0 <= i + by < devices]
    return lax.ppermute(array, axis, pairs)


def conv_forward(inputs, kernel, size, stride):
    channels = kernel.shape[0] // (size * size)
    shaped = kernel.reshape(channels, size, size, kernel.shape[1])
    return lax.conv_general_dilated(
        inputs,
        shaped,
        (stride, stride),
        "VALID",
        dimension_numbers=("NCHW", "IHWO", "NCHW"),
        preferred_element_type=jnp.float32,
    )


def conv_input_grad(upstream, kernel, size, stride):
    channels = kernel.shape[0] // (size * size)
    shaped = kernel.reshape(channels, size, size, kernel.shape[1])[:, ::-1, ::-1, :]
    border = ((size - 1, size - 1), (size - 1, size - 1))
    return lax.conv_general_dilated(
        upstream,
        shaped,
        (1, 1),
        border,
        lhs_dilation=(stride, stride),
        dimension_numbers=("NCHW", "OHWI", "NCHW"),
        preferred_element_type=jnp.float32,
    )


def conv_weight_grad(inputs, upstream, stride):
    result = lax.conv_general_dilated(
        inputs,
        upstream,
        (1, 1),
        "VALID",
        rhs_dilation=(stride, stride),
        dimension_numbers=("CNHW", "IOHW", "NHWC"),
        preferred_element_type=jnp.float32,
    )
    return result.reshape(-1, upstream.shape[1])


def contract(left, right, left_dim, right_dim):
    return lax.dot_general(
        left, right, (((left_dim,), (right_dim,)), ((), ())), preferred_element_type=jnp.float32
    )


def silu_slope(pre):
    sigmoid = jax.nn.sigmoid(pre)
    return sigmoid * (1.0 + pre * (1.0 - sigmoid))


def project_target(next_probs, rewards, discounts):
    support = -10.0 + 20.0 / (ATOMS - 1) * jnp.arange(ATOMS).astype(jnp.float32)
    moved = jnp.clip(rewards[:, None] + discounts[:, None] * support[None, :], -10.0, 10.0)
    place = (moved + 10.0) * ((ATOMS - 1) / 20.0)
    nodes = jnp.arange(ATOMS).astype(jnp.float32)
    spread = jnp.maximum(0.0, 1.0 - jnp.abs(place[:, :, None] - nodes[None, None, :]))
    return jnp.sum(next_probs[:, :, None] * spread, axis=1)


def action_mask(actions_row, dtype):
    return (jnp.arange(ACTIONS)[None, :] == actions_row[:, None]).astype(dtype)


def on_device(
    frames,
    conv1_weight,
    conv1_bias,
    conv2_weight,
    conv2_bias,
    conv3_weight,
    conv3_bias,
    dense_weight,
    dense_bias,
    head_weight,
    head_bias,
    taken_actions,
    next_actions,
    rewards,
    discounts,
    importance,
    buffer_slots,
):
    role = lax.axis_index("role")
    rows = frames.shape[1]
    kernel_one, kernel_two, kernel_three = (conv1_weight[0], conv2_weight[0], conv3_weight[0])
    dense_w, head_w = (dense_weight[0], head_weight[0])
    pixels = frames[0].astype(jnp.bfloat16).reshape(rows, STACK, SIDE, SIDE)
    pre_one = conv_forward(pixels, kernel_one, 8, 4) + conv1_bias[0][None, :, None, None]
    act_one = jax.nn.silu(pre_one).astype(jnp.bfloat16)
    pre_two = conv_forward(act_one, kernel_two, 4, 2) + conv2_bias[0][None, :, None, None]
    act_two = jax.nn.silu(pre_two).astype(jnp.bfloat16)
    pre_three = conv_forward(act_two, kernel_three, 3, 1) + conv3_bias[0][None, :, None, None]
    act_three = jax.nn.silu(pre_three).astype(jnp.bfloat16)
    features = act_three.reshape(rows, -1)
    pre_four = jnp.dot(features, dense_w, preferred_element_type=jnp.float32) + dense_bias[0]
    act_four = jax.nn.silu(pre_four).astype(jnp.bfloat16)
    logits = (jnp.dot(act_four, head_w, preferred_element_type=jnp.float32) + head_bias[0]).reshape(
        rows, ACTIONS, ATOMS
    )
    selected = jnp.where(role == 0, taken_actions, next_actions)
    chosen = jnp.sum(logits * action_mask(selected, jnp.float32)[:, :, None], axis=1)
    top = jnp.max(chosen, axis=1, keepdims=True)
    shifted = chosen - top
    exps = jnp.exp(shifted)
    sums = jnp.sum(exps, axis=1, keepdims=True)
    own_probs = exps / sums
    next_probs = shifted_2(own_probs, "role", -1)
    total = lax.psum(jnp.sum(importance), "batch")

    def run_backward():
        projected = project_target(next_probs, rewards, discounts)
        log_probs = shifted - jnp.log(sums)
        row_loss = -jnp.sum(projected * log_probs, axis=1)
        scaled = (importance / total)[:, None]
        delta = (
            scaled * (own_probs * jnp.sum(projected, axis=1, keepdims=True) - projected)
        ).astype(jnp.bfloat16)
        delta_full = (
            action_mask(taken_actions, jnp.bfloat16)[:, :, None] * delta[:, None, :]
        ).reshape(rows, -1)
        back_four = contract(delta_full, head_w, 1, 1)
        grad_four = (back_four * silu_slope(pre_four)).astype(jnp.bfloat16)
        dense_wg = contract(features, grad_four, 0, 0)
        dense_bg = jnp.sum(grad_four.astype(jnp.float32), axis=0)
        back_three = contract(grad_four, dense_w, 1, 1).reshape(pre_three.shape)
        grad_three = (back_three * silu_slope(pre_three)).astype(jnp.bfloat16)
        three_wg = conv_weight_grad(act_two, grad_three, 1)
        three_bg = jnp.sum(grad_three.astype(jnp.float32), axis=(0, 2, 3))
        back_two = conv_input_grad(grad_three, kernel_three, 3, 1)
        grad_two = (back_two * silu_slope(pre_two)).astype(jnp.bfloat16)
        two_wg = conv_weight_grad(act_one, grad_two, 2)
        two_bg = jnp.sum(grad_two.astype(jnp.float32), axis=(0, 2, 3))
        back_one = conv_input_grad(grad_two, kernel_two, 4, 2)
        grad_one = (back_one * silu_slope(pre_one)).astype(jnp.bfloat16)
        one_wg = conv_weight_grad(pixels, grad_one, 4)
        one_bg = jnp.sum(grad_one.astype(jnp.float32), axis=(0, 2, 3))
        return (
            one_wg,
            one_bg,
            two_wg,
            two_bg,
            three_wg,
            three_bg,
            dense_wg,
            dense_bg,
            grad_one,
            delta,
            row_loss,
        )

    def skip_backward():
        return (
            jnp.zeros(kernel_one.shape, jnp.float32),
            jnp.zeros(conv1_bias.shape[1:], jnp.float32),
            jnp.zeros(kernel_two.shape, jnp.float32),
            jnp.zeros(conv2_bias.shape[1:], jnp.float32),
            jnp.zeros(kernel_three.shape, jnp.float32),
            jnp.zeros(conv3_bias.shape[1:], jnp.float32),
            jnp.zeros(dense_w.shape, jnp.float32),
            jnp.zeros(dense_bias.shape[1:], jnp.float32),
            jnp.zeros(pre_one.shape, jnp.bfloat16),
            jnp.zeros((rows, ATOMS), jnp.bfloat16),
            jnp.zeros((rows,), jnp.float32),
        )

    (
        one_wg,
        one_bg,
        two_wg,
        two_bg,
        three_wg,
        three_bg,
        dense_wg,
        dense_bg,
        grad_one,
        delta,
        row_loss,
    ) = lax.cond(role == 0, run_backward, skip_backward)
    hidden_in, delta_in = shifted_2((act_four, delta), "role", 1)
    delta_wide = (
        action_mask(taken_actions, jnp.bfloat16)[:, :, None] * delta_in[:, None, :]
    ).reshape(rows, -1)
    head_wg = contract(hidden_in, delta_wide, 0, 0)
    head_bg = jnp.sum(delta_wide.astype(jnp.float32), axis=0)
    grad_landed, kernel_landed = shifted_2((grad_one, kernel_one), "role", 1)
    grad_pick = jnp.where(role == 0, grad_one, grad_landed)
    kernel_pick = jnp.where(role == 0, kernel_one, kernel_landed)
    per_half = STACK // lax.axis_size("role")
    kernel_half = lax.dynamic_slice_in_dim(kernel_pick, role * per_half * 64, per_half * 64, 0)
    frame_part = conv_input_grad(grad_pick, kernel_half, 8, 4).reshape(rows, per_half, SIDE * SIDE)
    outputs = lax.psum(
        (one_wg, one_bg, two_wg, two_bg, three_wg, three_bg, dense_wg, dense_bg, head_wg, head_bg),
        ("role", "batch"),
    )
    slot_count = rows * lax.axis_size("batch")
    spread_loss = jnp.zeros((slot_count,), jnp.float32).at[buffer_slots].add(row_loss)
    priorities = lax.psum_scatter(spread_loss, ("role", "batch"), scatter_dimension=0, tiled=True)
    return (
        frame_part,
        outputs[0],
        outputs[1],
        outputs[2],
        outputs[3],
        outputs[4],
        outputs[5],
        outputs[6],
        outputs[7],
        outputs[8],
        outputs[9],
        priorities,
    )


def solution(mesh):
    in_specs = (
        P("role", "batch", None, None),
        P("role", None, None),
        P("role", None),
        P("role", None, None),
        P("role", None),
        P("role", None, None),
        P("role", None),
        P("role", None, None),
        P("role", None),
        P("role", None, None),
        P("role", None),
        P("batch"),
        P("batch"),
        P("batch"),
        P("batch"),
        P("batch"),
        P("batch"),
    )
    out_specs = (
        P("batch", "role", None),
        P(),
        P(),
        P(),
        P(),
        P(),
        P(),
        P(),
        P(),
        P(),
        P(),
        P(("role", "batch")),
    )
    return jax.shard_map(
        on_device, mesh=mesh, in_specs=in_specs, out_specs=out_specs, check_vma=False
    )
```

profile of v0, /device:TPU:14, one launch (start us, length us, event | category | flops | bytes accessed | tf_op | source)
XLA Modules:
  0.0 621.4 jit_solution(12637567262641721012)
XLA Ops:
  8.1 13.9 %convert_element_type.89 = bf16[1,224,4,7056]{3,2,1,0:T(4,128)(2,1)} convert(f32[1,224,4,7056]{3,2,1,0:T(4,128)} %param.19) | non-fusion elementwise | flops 6322176 | bytes 37933056 | tf_op jit(solution)/shard_map/convert_element_type | solution.py:106
  22.0 30.0 %copy.111 = bf16[1,224,4,7056]{1,2,3,0:T(4,128)(2,1)} copy(bf16[1,224,4,7056]{3,2,1,0:T(4,128)(2,1)} %convert_element_type.89) | data formatting | bytes 25288704 | tf_op jit(solution)/shard_map/convert_element_type | solution.py:106
  52.5 21.0 %multiply_convert_fusion.3 = (bf16[224,32,20,20]{0,1,3,2:T(8,128)(2,1)}, f32[224,32,20,20]{0,1,3,2:T(8,128)}) fusion(f32[32]{0:T(128)S(1)} %bitcast.68, bf16[224,4,84,84]{0,1,3,2:T(4,128)(2,1)} %bitcast.56, bf16[4,8,8,32]{3,2,1,0:T(8,128)(2,1)S(1)} %bitcast.60), kind=kOutput, calls=%fused_computation.36 | convolution fusion | flops 1485209600 | bytes 29864064 | tf_op jit(solution)/shard_map/conv_general_dilated | solution.py:21
  73.5 9.2 %broadcast_add_fusion = (f32[224,64,9,9]{0,1,3,2:T(8,128)}, bf16[224,64,9,9]{0,1,3,2:T(8,128)(2,1)S(1)}) fusion(f32[64]{0:T(128)S(1)} %bitcast.69, bf16[224,32,20,20]{0,1,3,2:T(8,128)(2,1)} %get-tuple-element.263, bf16[32,4,4,64]{3,2,1,0:T(4,128)(2,1)S(1)} %bitcast.64), kind=kOutput, calls=%fused_computation.43 | convolution fusion | flops 1196052480 | bytes 12767488 | tf_op jit(solution)/shard_map/conv_general_dilated | solution.py:21
  82.7 5.0 multiply_convert_fusion.5
  89.6 3.8 broadcast_add_fusion.1
  94.1 1.2 copy.120
  95.3 1.3 reshape.194
  96.9 2.5 collective-permute-start
  99.9 21.4 %psum.77 = f32[]{:T(128)} all-reduce(f32[]{:T(128)} %reduce_sum.101), channel_id=1, replica_groups=mesh['role'=2,'batch'=16] {'batch'}, use_global_device_ids=true, to_apply=%region_4.5 | all-reduce | flops 1 | bytes 8 | tf_op jit(solution)/shard_map/psum | solution.py:127
  121.3 1.5 copy.119
  122.9 15.1 %conditional.1 = (f32[256,32]{1,0:T(8,128)}, f32[32]{0:T(128)}, f32[512,64]{1,0:T(8,128)}, f32[64]{0:T(128)}, f32[576,64]{1,0:T(8,128)}, /*index=5*/f32[64]{0:T(...) conditional(s32[]{:T(128)} %convert_element_type.88, () %tuple.16, ...), branch_computations={%region_5.6_spmd, %region_6.14_spmd} | conditional | flops 7171585536 | bytes 154460032 | solution.py:197
  126.6 3.6 broadcast.160
  130.2 3.5 broadcast.162
  138.0 1.3 collective-permute-start.1
  139.3 1.3 collective-permute-start.3
  140.6 1.3 collective-permute-start.2
  141.9 1.3 collective-permute-start.4
  143.2 214.6 %collective-permute-done.2 = bf16[256,32]{1,0:T(8,128)(2,1)S(1)} collective-permute-done((bf16[256,32]{1,0:T(8,128)(2,1)}, bf16[256,32]{1,0:T(8,128)(2,1)S(1)}, u32[]{:S(2)}, u32[]{:S(2)}) %collective-permute-start.2) | collective-permute-done | bytes 16416 | tf_op jit(solution)/shard_map/ppermute | solution.py:15
  358.6 1.0 copy.127
  359.6 1.7 copy.128
  361.3 1.8 copy.129
  363.1 1.9 scatter_custom_fusion
  365.6 48.4 %all-reduce.1 = (f32[256,32]{0,1:T(8,128)}, f32[32]{0:T(128)}, f32[64]{0:T(128)}, f32[64]{0:T(128)}, f32[512]{0:T(512)}, /*index=5*/f32[918]{0:T(1024)}, f32[3584]{0:T(1024)S(1)}) all-reduce(f32[256,32]{0,1:T(8,128)S(1)} %copy.127, f32[32]{0:T(128)} %get-tuple-element.88, ...), channel_id=1, replica_groups=mesh['role'=2,'batch'=16] {'role','batch'}, use_global_device_ids=true, to_apply=%region_14.15 | all-reduce | flops 13366 | bytes 106928 | tf_op jit(solution)/shard_map/psum | solution.py:210
  414.5 1.6 fusion.39
  416.2 6.9 %fusion.62 = bf16[224,32,20,20]{0,1,3,2:T(8,128)(2,1)} fusion(bf16[224,32,20,20]{0,1,3,2:T(8,128)(2,1)} %get-tuple-element.86, bf16[224,32,20,20]{0,1,3,2:T(8,128)(2,1)} %collective-permute-done.1, pred[]{:T(512)S(6)} %eq.57), kind=kLoop, calls=%fused_computation.39.clone.1 | loop fusion | flops 2867200 | bytes 17203200 | tf_op jit(solution)/shard_map/conv_general_dilated | solution.py:35
  423.1 153.9 %fusion.16 = f32[224,2,84,84]{0,1,3,2:T(2,128)} fusion(bf16[2,8,8,32]{3,2,1,0:T(8,128)(2,1)S(1)} %bitcast.63, bf16[224,32,20,20]{0,1,3,2:T(8,128)(2,1)} %fusion.62), kind=kOutput, calls=%fused_computation.38 | convolution fusion | flops 734003200 | bytes 18386944 | tf_op jit(solution)/shard_map/conv_general_dilated | solution.py:35
  577.0 26.5 %copy.130 = f32[224,2,7056]{2,1,0:T(2,128)} copy(f32[224,2,7056]{0,1,2:T(2,128)} %bitcast.55) | data formatting | bytes 25288704
  603.5 1.6 copy.207
  605.1 1.6 copy.208
  606.7 6.4 %copy.209 = f32[3136,512]{1,0:T(8,128)} copy(f32[3136,512]{1,0:T(8,128)} %get-tuple-element.296) | data formatting | bytes 12845056
  613.1 1.2 copy.210
  (76 shorter events, 10.9 us)
Async XLA Ops:
  7.2 596.3 %all-reduce.5.cloned.1.call-start = ((), (), s32[]{:S(2)}) async-start(), calls=%async_computation | async-start | bytes 17203200 | tf_op jit(solution)/shard_map/psum | solution.py:210
  8.1 44.4 %copy-start.12 = (bf16[1,256,32]{2,1,0:T(8,128)(2,1)}, bf16[1,256,32]{2,1,0:T(8,128)(2,1)S(1)}, u32[]{:S(2)}) copy-start(bf16[1,256,32]{2,1,0:T(8,128)(2,1)S(1)} %copy.112) | copy-start | bytes 49156
  22.0 30.0 %copy-start.8 = (bf16[1,512,64]{1,2,0:T(8,128)(2,1)S(1)}, bf16[1,512,64]{1,2,0:T(8,128)(2,1)}, u32[]{:S(2)}) copy-start(bf16[1,512,64]{1,2,0:T(8,128)(2,1)} %param.22) | copy-start | bytes 196612
  22.0 30.1 %copy-start.6 = (bf16[1,576,64]{1,2,0:T(8,128)(2,1)S(1)}, bf16[1,576,64]{1,2,0:T(8,128)(2,1)}, u32[]{:S(2)}) copy-start(bf16[1,576,64]{1,2,0:T(8,128)(2,1)} %param.24) | copy-start | bytes 221188
  22.0 30.4 %copy-start.23 = (f32[1,32]{1,0:T(1,128)S(1)}, f32[1,32]{1,0:T(1,128)}, u32[]{:S(2)}) copy-start(f32[1,32]{1,0:T(1,128)} %param.21) | copy-start | bytes 388
  52.4 21.0 %copy-start.24 = (f32[1,64]{1,0:T(1,128)S(1)}, f32[1,64]{1,0:T(1,128)}, u32[]{:S(2)}) copy-start(f32[1,64]{1,0:T(1,128)} %param.23) | copy-start | bytes 772
  73.4 9.3 %copy-start.25 = (f32[1,64]{1,0:T(1,128)S(1)}, f32[1,64]{1,0:T(1,128)}, u32[]{:S(2)}) copy-start(f32[1,64]{1,0:T(1,128)} %param.25) | copy-start | bytes 772
  82.7 5.0 copy-start.27
  87.7 1.9 copy-start.22
  88.6 4.8 copy-start.16
  89.6 3.8 copy-start.2
  89.6 7.0 %copy-start.15 = (s32[224]{0:T(256)S(1)}, s32[224]{0:T(256)}, u32[]{:S(2)}) copy-start(s32[224]{0:T(256)} %param.30) | copy-start | bytes 2692
  89.6 7.0 %copy-start.18 = (s32[224]{0:T(256)S(1)}, s32[224]{0:T(256)}, u32[]{:S(2)}) copy-start(s32[224]{0:T(256)} %param.31) | copy-start | bytes 2692
  93.4 0.7 copy-start.10
  93.4 6.0 copy-start.17
  93.4 29.5 %copy-start.7 = (bf16[1,576,64]{1,2,0:T(8,128)(2,1)S(1)}, bf16[1,576,64]{1,2,0:T(8,128)(2,1)}, u32[]{:S(2)}) copy-start(bf16[1,576,64]{1,2,0:T(8,128)(2,1)} %param.24) | copy-start | bytes 221188
  93.4 29.5 %copy-start.20 = (f32[224]{0:T(256)S(1)}, f32[224]{0:T(256)}, u32[]{:S(2)}) copy-start(f32[224]{0:T(256)} %param.32) | copy-start | bytes 2692
  93.4 29.5 %copy-start.21 = (f32[224]{0:T(256)S(1)}, f32[224]{0:T(256)}, u32[]{:S(2)}) copy-start(f32[224]{0:T(256)} %param.33) | copy-start | bytes 2692
  96.9 26.0 %collective-permute-start = (f32[224,51]{0,1:T(8,128)S(1)}, f32[224,51]{0,1:T(8,128)S(1)}, u32[]{:S(2)}, u32[]{:S(2)}) collective-permute-start(f32[224,51]{0,1:T(8,128)S(1)} %exponential_divide_fusion), channel_id=1, source_target_pairs={{16,0},{17,1},{18,2},{19,3},{20,4},{21,5},{22,6},{23,7},{24,8},{25... | collective-permute-start | bytes 137096 | tf_op jit(solution)/shard_map/ppermute | solution.py:15
  122.9 19.1 %copy-start.19 = (s32[224]{0:T(256)S(1)}, s32[224]{0:T(256)}, u32[]{:S(2)}) copy-start(s32[224]{0:T(256)} %param.35) | copy-start | bytes 2692
  138.0 278.2 %collective-permute-start.1 = (bf16[224,32,20,20]{0,1,3,2:T(8,128)(2,1)}, bf16[224,32,20,20]{0,1,3,2:T(8,128)(2,1)}, u32[]{:S(2)}, u32[]{:S(2)}) collective-permute-start(bf16[224,32,20,20]{0,1,3,2:T(8,128)(2,1)} %get-tuple-element.86), channel_id=1, source_target_pairs={{0,16},{1,17},{2,18},{3,19},{4,20},{5,21},{6,22},{7,23},{8,24},{9,... | collective-permute-start | bytes 17203208 | tf_op jit(solution)/shard_map/ppermute | solution.py:15
  139.3 275.2 %collective-permute-start.3 = (bf16[224,512]{1,0:T(8,128)(2,1)}, bf16[224,512]{1,0:T(8,128)(2,1)S(1)}, u32[]{:S(2)}, u32[]{:S(2)}) collective-permute-start(bf16[224,512]{1,0:T(8,128)(2,1)} %copy-done.10), channel_id=1, source_target_pairs={{0,16},{1,17},{2,18},{3,19},{4,20},{5,21},{6,22},{7,23},{8,24},{9,... | collective-permute-start | bytes 688136 | tf_op jit(solution)/shard_map/ppermute | solution.py:15
  140.6 217.2 %collective-permute-start.2 = (bf16[256,32]{1,0:T(8,128)(2,1)}, bf16[256,32]{1,0:T(8,128)(2,1)S(1)}, u32[]{:S(2)}, u32[]{:S(2)}) collective-permute-start(bf16[256,32]{1,0:T(8,128)(2,1)} %bitcast.61), channel_id=1, source_target_pairs={{0,16},{1,17},{2,18},{3,19},{4,20},{5,21},{6,22},{7,23},{8,24},{9,... | collective-permute-start | bytes 49160 | tf_op jit(solution)/shard_map/ppermute | solution.py:15
  141.9 223.1 %collective-permute-start.4 = (bf16[224,51]{0,1:T(8,128)(2,1)S(1)}, bf16[224,51]{0,1:T(8,128)(2,1)S(1)}, u32[]{:S(2)}, u32[]{:S(2)}) collective-permute-start(bf16[224,51]{0,1:T(8,128)(2,1)S(1)} %get-tuple-element.95), channel_id=1, source_target_pairs={{0,16},{1,17},{2,18},{3,19},{4,20},{5,21},{6,22},{7,23},{8,24},{9,... | collective-permute-start | bytes 68552 | tf_op jit(solution)/shard_map/ppermute | solution.py:15
  606.7 6.4 %copy-start.4 = (f32[512,918]{0,1:T(8,128)S(1)}, f32[512,918]{0,1:T(8,128)}, u32[]{:S(2)}) copy-start(f32[512,918]{0,1:T(8,128)} %get-tuple-element.298) | copy-start | bytes 5640196
Sparse Core Ops, SparseCore 0:
  416.3 182.1 all-reduce.4
where the time goes:
time: 628 us; the launch traced here: 621 us
  waiting for transfers between devices  215 us (34%)
  matrix products  195 us (31%)
  local copies, waits for them, and re-layouts  91.4 us (15%)
  blocking collectives  69.7 us (11%)
  other arithmetic  24.6 us (4%)
  between operations  14.7 us (2%)
  starting transfers between devices  7.68 us (1%)
    ppermute x5, waiting for transfers between devices, shifted_2(): return lax.ppermute(array, axis, pairs)  215 us
    conv_general_dilated x1, matrix products, conv_input_grad(): lax.conv_general_dilated(upstream, shaped, (1, 1), border, lhs_dilation=(...  154 us
    psum x1, blocking collectives, on_device(): lax.psum((one_wg, one_bg, two_wg, two_bg, three_wg, three_bg, dense_wg, d...  48.4 us
    unnamed x48, local copies, waits for them, and re-layouts  40.7 us
    conv_general_dilated x3, matrix products, conv_forward(): lax.conv_general_dilated(inputs, shaped, (stride, stride), 'VALID', dimen...  35.2 us
    convert_element_type x1, local copies, waits for them, and re-layouts, on_device(): pixels = frames[0].astype(jnp.bfloat16).reshape(rows, STACK, SIDE, SIDE)  30 us
    psum x1, blocking collectives, on_device(): total = lax.psum(jnp.sum(importance), 'batch')  21.4 us
    convert_element_type x1, other arithmetic, on_device(): pixels = frames[0].astype(jnp.bfloat16).reshape(rows, STACK, SIDE, SIDE)  13.9 us
  transfers between devices with their start and end apart: 6, of which 1 were waited for; matrix products, arithmetic and copies ran while one was open for 32% of the time, Pallas kernels for 0%

commit v1 on v0

v1 whole, which is shorter than its diff:
```python
import functools

import jax
import jax.numpy as jnp
import numpy as np
from jax import lax
from jax.experimental import pallas as pl
from jax.experimental.pallas import tpu as pltpu
from jax.sharding import PartitionSpec as P

STACK = 4
SIDE = 84
ACTIONS = 18
ATOMS = 51
LOGITS = ACTIONS * ATOMS
PIX = SIDE * SIDE
BAND = 4 * SIDE
WIDE = 384
TILES = 56
SUB = 32
F32 = jnp.float32
BF16 = jnp.bfloat16
HIGHEST = lax.Precision.HIGHEST
MESH = pl.DeviceIdType.MESH

NN = (((1,), (0,)), ((), ()))
NT = (((1,), (1,)), ((), ()))
TN = (((0,), (0,)), ((), ()))

ROW_HEAD = 3136
ROW_TWO = ROW_HEAD + 928
ROW_THREE = ROW_TWO + 64
ROW_THREE_REST = ROW_THREE + 64
ROW_ONE = ROW_THREE_REST + 64
ROW_BIAS = ROW_ONE + 32
ROW_LOSS = ROW_BIAS + 16


def dot(left, right, dims=NN, precision=None):
    return lax.dot_general(left, right, dims, precision=precision, preferred_element_type=F32)


def iota(shape, dim):
    return lax.broadcasted_iota(jnp.int32, shape, dim)


def onehot(condition, dtype):
    return jnp.where(condition, 1.0, 0.0).astype(dtype)


def silu_and_slope(pre):
    gate = 0.5 * jnp.tanh(0.5 * pre) + 0.5
    act = pre * gate
    return act.astype(BF16), gate + act * (1.0 - gate)


def tall(value):
    return value.reshape(value.shape[0] * value.shape[1], value.shape[2])


class Plan:
    def __init__(self, batch, slots):
        self.batch = batch
        self.bits = batch.bit_length() - 1
        if 1 << self.bits != batch:
            raise ValueError("batch axis")
        self.loss_rows = -(-slots // (512 * 16)) * 16
        unit = 16 * batch
        units = -(-(ROW_LOSS + self.loss_rows) // unit)
        self.rows = units * unit
        count = min(4, units)
        up = list(range(self.bits))
        round_way = up[:1] + up[2:] + up[1:2]
        self.streams, at = [], 0
        for s in range(count):
            size = (units // count + (1 if s < units % count else 0)) * unit
            self.streams.append((at, size, up if s % 2 == 0 else round_way))
            at += size


def banded_first(kernel_t, channel, line, column, real, channels, lanes):
    rows = channel.shape[0]
    spread = onehot((iota((lanes, 32), 0) & 31) == iota((lanes, 32), 1), BF16)
    tiled = dot(spread, kernel_t).astype(BF16)
    block, rest = column >> 2, column & 3
    lane_x = iota((rows, lanes), 1) >> 5
    found = []
    for half in range(2):
        parts = []
        for step in range(2):
            goal = jnp.where(real, channel * 64 + (4 * half + line) * 8 + 4 * step + rest, -1)
            pick = onehot(iota((rows, channels * 64), 1) == goal, BF16)
            parts.append(dot(pick, tiled, NT))
        found.append(jnp.where(lane_x == block, parts[0], jnp.where(lane_x == block - 1, parts[1], 0.0)).astype(BF16))
    return found


def build_first(kernel_t, out):
    row = iota((512, 1), 0)
    found = banded_first(kernel_t, row >> 7, (row >> 5) & 3, row & 31, row >= 0, STACK, 224)
    for half in range(2):
        out[half] = found[half]


def build_frame(kernel_t, out):
    row = iota((2 * WIDE, 1), 0)
    channel = (row >= WIDE).astype(jnp.int32)
    inner = row - channel * WIDE
    line = sum((inner >= SIDE * i).astype(jnp.int32) for i in range(1, 5))
    found = banded_first(kernel_t, channel, line, inner - line * SIDE, line < 4, 2, 640)
    for half in range(2):
        out[half] = found[half]


def build_second(kernel_t, out):
    goal = (iota((512, 512), 0) & 31) * 16 + (iota((512, 512), 0) >> 5)
    by_place = dot(onehot(iota((512, 512), 1) == goal, BF16), kernel_t, NT).astype(BF16)
    out[...] = jnp.zeros_like(out)
    for ky in range(4):
        for kx in range(4):
            piece = by_place[(ky * 4 + kx) * 32 : (ky * 4 + kx + 1) * 32]
            for x in range(3):
                low = 256 * ky + (2 * x + kx) * 32
                out[low : low + 32, 64 * x : 64 * x + 64] = piece


def build_third(kernel_t, tall_out, wide_out):
    goal = (iota((576, 576), 0) & 63) * 9 + (iota((576, 576), 0) >> 6)
    by_place = dot(onehot(iota((576, 576), 1) == goal, BF16), kernel_t, NT).astype(BF16)
    tall_out[...] = jnp.zeros_like(tall_out)
    wide_out[...] = jnp.zeros_like(wide_out)
    for ky in range(3):
        for kx in range(3):
            piece = by_place[(ky * 3 + kx) * 64 : (ky * 3 + kx + 1) * 64]
            for x in range(2):
                low = (x + kx) * 64
                tall_out[256 * ky + low : 256 * ky + low + 64, 64 * x : 64 * x + 64] = piece
                wide_out[low : low + 64, 128 * ky + 64 * x : 128 * ky + 64 * x + 64] = piece


def build_picks(out):
    lane = iota((1, WIDE), 1)
    group, line, column = lane >> 7, (lane >> 5) & 3, lane & 31
    goal = jnp.where(28 * group + column < SIDE, SIDE * line + 28 * group + column, -1000)
    row = iota((512, WIDE), 0)
    for kind in range(8):
        out[512 * kind : 512 * kind + 512, :WIDE] = onehot(row == goal + (BAND * kind) % 128, BF16)


def core_kernel(plan, steps, *refs):
    (x_hbm, edge, k1_ref, k2_ref, k3_ref, w4_hbm, b1_ref, b2_ref, b3_ref, b4, w5, b5, cols, lane_action, compact) = refs[:15]
    frame_out, dense_out, sums_out = refs[15:18]
    (
        raw, lines, x, a1, s1, a2, s2, a3, s3, a4, g4, delta_all, g1, pad2, pad3, acc, band_k,
        k1, k2, k3, k3_wide, w4, bias, acc1, acc2, acc3, bias_sums, loss_sums, send, landed, final, probs_all, logp, nexts,
        totals, totals_in, k1_online,
        raw_sem, w4_sem, tile_sem, probs_send, probs_recv, g1_send, g1_recv, tot_send, tot_recv, k1_send, k1_recv,
        rs_send, rs_recv, ag_send, ag_recv, x_send, x_recv, out_sem,
    ) = refs[18:]
    role, place = lax.axis_index("role"), lax.axis_index("batch")
    online = role == 0

    def bit_of(bit):
        return (place // (1 << bit)) % 2

    def across(bit):
        return {"batch": place + (1 - 2 * bit_of(bit)) * (1 << bit)}

    other_role = {"role": 1 - role}

    def remote(src, dst, send_sem, recv_sem, device):
        return pltpu.make_async_remote_copy(
            src_ref=src, dst_ref=dst, send_sem=send_sem, recv_sem=recv_sem, device_id=device, device_id_type=MESH
        )

    def raw_copies(step, slot):
        return [
            pltpu.make_async_copy(
                x_hbm.at[0, pl.ds(step * SUB, SUB), :, pl.ds(128 * t, 128)], raw.at[slot, t], raw_sem.at[slot]
            )
            for t in range(TILES - 1)
        ]

    weight_copy = pltpu.make_async_copy(w4_hbm, send.at[pl.ds(0, 3136)], w4_sem)
    weight_copy.start()
    for c in raw_copies(0, 0):
        c.start()

    barrier = pltpu.get_barrier_semaphore()
    for bit in range(plan.bits):
        pl.semaphore_signal(barrier, inc=1, device_id=across(bit), device_id_type=MESH)
    pl.semaphore_signal(barrier, inc=1, device_id=other_role, device_id_type=MESH)
    pl.semaphore_wait(barrier, plan.bits + 1)

    kernel_copy = remote(k1_ref, k1_online, k1_send, k1_recv, other_role)

    @pl.when(online)
    def _():
        kernel_copy.start()

    totals[0] = jnp.broadcast_to(jnp.sum(cols[:, 2:3], axis=0, keepdims=True), (8, 128))

    def total_copy(stage):
        return remote(totals.at[stage], totals_in.at[stage], tot_send.at[stage], tot_recv.at[stage], across(stage))

    def total_step(stage):
        if stage > 0:
            total_copy(stage - 1).wait_recv()
            totals[stage] = totals[stage - 1] + totals_in[stage - 1]
        if stage < plan.bits:
            total_copy(stage).start()

    todo = list(range(plan.bits + 1))
    total_step(todo.pop(0))
    build_first(k1_ref[...], k1)
    total_step(todo.pop(0))
    build_second(k2_ref[...], k2)
    if len(todo) > 1:
        total_step(todo.pop(0))
    build_third(k3_ref[...], k3, k3_wide)
    if len(todo) > 1:
        total_step(todo.pop(0))
    bias[...] = jnp.zeros_like(bias)
    for at, (ref, size, copies) in enumerate(((b1_ref, 32, 20), (b2_ref, 64, 9), (b3_ref, 64, 7))):
        repeat = onehot((iota((size, size * copies), 1) & (size - 1)) == iota((size, size * copies), 0), F32)
        bias[at : at + 1, : size * copies] = dot(ref[...], repeat, precision=HIGHEST)
    acc1[...] = jnp.zeros_like(acc1)
    acc2[...] = jnp.zeros_like(acc2)
    acc3[...] = jnp.zeros_like(acc3)
    bias_sums[...] = jnp.zeros_like(bias_sums)
    loss_sums[...] = jnp.zeros_like(loss_sums)
    pad3[...] = jnp.zeros_like(pad3)
    pad2[...] = jnp.zeros_like(pad2)
    a2[...] = jnp.zeros_like(a2)
    for step in range(steps):
        g1[step, 0] = jnp.zeros((SUB, 640), BF16)
        g1[step, 21] = jnp.zeros((SUB, 640), BF16)
    weight_copy.wait()
    spare = raw.reshape(2, (TILES - 1) * SUB * STACK, 128)
    for pair in range(2):
        for q in range(2):
            low = 128 * (2 * pair + q)
            spare[1, 3136 * q : 3136 * q + 3136] = send[:3136, low : low + 128].astype(F32)
        for spot in range(49):
            for q in range(2):
                low = 128 * (2 * pair + q)
                w4[64 * spot : 64 * spot + 64, low : low + 128] = spare[
                    1, pl.ds(3136 * q + spot, 64, stride=49), :
                ].astype(BF16)
    build_picks(send)
    while todo:
        total_step(todo.pop(0))
    for stage in range(plan.bits):
        total_copy(stage).wait_send()

    raw_flat = raw.reshape(2, TILES - 1, SUB * STACK, 128)

    def forward(step, slot):
        rows = pl.ds(pl.multiple_of(step * SUB, SUB), SUB)
        own = cols[rows, :]
        for kind in range(8):
            bands = list(range(kind, 21, 8))
            for at, band in enumerate(bands):
                low = BAND * band // 128
                for c in range(STACK):
                    place_at = (at * STACK + c) * SUB
                    for t in range(4):
                        if low + t < TILES - 1:
                            piece = raw_flat[slot, low + t, pl.ds(c, SUB, stride=STACK), :]
                        else:
                            piece = edge[pl.ds(step * (SUB * STACK) + c, SUB, stride=STACK), :]
                        lines[place_at : place_at + SUB, 128 * t : 128 * t + 128] = piece.astype(BF16)
            count = len(bands) * STACK * SUB
            sorted_lines = dot(lines[:count], send[512 * kind : 512 * kind + 512, :WIDE]).astype(BF16)
            for at, band in enumerate(bands):
                for c in range(STACK):
                    place_at = (at * STACK + c) * SUB
                    for group in range(3):
                        x[band, :, 512 * group + 128 * c : 512 * group + 128 * c + 128] = sorted_lines[
                            place_at : place_at + SUB, 128 * group : 128 * group + 128
                        ]
        for group, lanes in enumerate((224, 224, 192)):
            part = tall(x[:, :, 512 * group : 512 * group + 512])
            acc[: 20 * SUB, 224 * group : 224 * group + lanes] = dot(part[: 20 * SUB], k1[0, :, :lanes]) + dot(
                part[SUB:], k1[1, :, :lanes]
            )
        for y in range(20):
            act, slope = silu_and_slope(acc[y * SUB : (y + 1) * SUB, :640] + bias[0:1, :640])
            a1[y % 2, y // 2] = act
            s1[y % 2, y // 2] = slope
        for group in range(3):
            even, odd = (tall(a1[p, :, :, 192 * group : 192 * group + 256]) for p in range(2))
            joined = jnp.concatenate([even[: 9 * SUB], odd[: 9 * SUB], even[SUB:], odd[SUB:]], axis=1)
            acc[: 9 * SUB, 192 * group : 192 * group + 192] = dot(joined, k2[...])
        for y in range(9):
            act, slope = silu_and_slope(acc[y * SUB : (y + 1) * SUB, :576] + bias[1:2, :576])
            a2[y, :, :576] = act
            s2[y] = slope
        for pair in range(4):
            low = 128 * pair
            joined = jnp.concatenate([tall(a2[ky : ky + 7, :, low : low + 256]) for ky in range(3)], axis=1)
            acc[: 7 * SUB, low : low + 128] = dot(joined, k3[...])
        pre4 = b4[...]
        for y in range(7):
            act, slope = silu_and_slope(acc[y * SUB : (y + 1) * SUB, :448] + bias[2:3, :448])
            a3[y, rows, :] = act
            s3[y] = slope
            pre4 = pre4 + dot(act, w4[448 * y : 448 * y + 448])
        act, slope4 = silu_and_slope(pre4)
        a4[rows, :] = act
        logits = dot(act, w5[...], NT) + b5[...]
        picked = jnp.where(lane_action[...] == own[:, 3:4], logits, 0.0)
        high = picked.astype(BF16)
        rest = picked - high.astype(F32)
        middle = rest.astype(BF16)
        low_part = (rest - middle.astype(F32)).astype(BF16)
        thrice = dot(jnp.concatenate([high, middle, low_part], axis=0), compact[...], NT)
        chosen = thrice[:SUB] + thrice[SUB : 2 * SUB] + thrice[2 * SUB :]
        real = iota((SUB, 128), 1) < ATOMS
        shifted = chosen - jnp.max(jnp.where(real, chosen, -jnp.inf), axis=1, keepdims=True)
        exps = jnp.where(real, jnp.exp(shifted), 0.0)
        sums = jnp.sum(exps, axis=1, keepdims=True)
        probs_all[step] = exps / sums
        logp[...] = jnp.where(real, shifted - jnp.log(sums), 0.0)
        return slope4

    def probs_copy(step):
        return remote(probs_all.at[step], nexts.at[step], probs_send.at[step], probs_recv.at[step], other_role)

    def grad_copy(step):
        return remote(g1.at[step, pl.ds(1, 20)], g1.at[step, pl.ds(1, 20)], g1_send.at[step], g1_recv.at[step], other_role)

    def backward(step, slope4):
        rows = pl.ds(pl.multiple_of(step * SUB, SUB), SUB)
        own = cols[rows, :]
        nodes = iota((SUB, 128), 1).astype(F32)
        reward, discount, importance = own[:, 0:1], own[:, 1:2], own[:, 2:3]
        support = -10.0 + 20.0 / (ATOMS - 1) * nodes
        spot = (jnp.clip(reward + discount * support, -10.0, 10.0) + 10.0) * ((ATOMS - 1) / 20.0)
        next_probs = nexts[step]
        projected = jnp.zeros((SUB, 128), F32)
        for j in range(ATOMS):
            projected += next_probs[:, j : j + 1] * jnp.maximum(0.0, 1.0 - jnp.abs(spot[:, j : j + 1] - nodes))
        projected = jnp.where(nodes < ATOMS, projected, 0.0)
        mass = jnp.sum(projected, axis=1, keepdims=True)
        row_loss = -jnp.sum(projected * logp[...], axis=1, keepdims=True)
        high = (row_loss * onehot(own[:, 5:6] == iota((SUB, plan.loss_rows), 1).astype(F32), F32)).astype(BF16)
        low = onehot(own[:, 6:7] == iota((SUB, 512), 1).astype(F32), BF16)
        loss_sums[...] += dot(high, low, TN)
        scaled = importance / totals[plan.bits, 0:1, 0:1]
        delta = (scaled * (probs_all[step] * mass - projected)).astype(BF16)
        spread = dot(delta, compact[...])
        delta_full = jnp.where(lane_action[...] == own[:, 4:5], spread, 0.0).astype(BF16)
        delta_all[rows, :] = delta_full
        grad4 = (dot(delta_full, w5[...]) * slope4).astype(BF16)
        g4[rows, :] = grad4
        for y in range(7):
            pad3[y + 2, :, :448] = (dot(grad4, w4[448 * y : 448 * y + 448], NT) * s3[y]).astype(BF16)
        for pair in range(4):
            low = 128 * pair
            joined = jnp.concatenate([tall(pad3[2 - ky : 11 - ky, :, low : low + 128]) for ky in range(3)], axis=1)
            total = dot(joined, k3_wide[...], NT)
            if pair == 0:
                acc[: 9 * SUB, :256] = total
            else:
                acc[: 9 * SUB, low : low + 128] += total[:, :128]
                acc[: 9 * SUB, low + 128 : low + 256] = total[:, 128:]
        for y in range(9):
            pad2[y + 1] = (acc[y * SUB : (y + 1) * SUB, :576] * s2[y]).astype(BF16)
        for parity in range(2):
            for group in range(3):
                low = 192 * group
                part = tall(pad2[:, :, low : low + 192])
                total = dot(part[SUB:], k2[256 * parity : 256 * parity + 256], NT) + dot(
                    part[: 10 * SUB], k2[256 * parity + 512 : 256 * parity + 768], NT
                )
                if group == 0:
                    acc[: 10 * SUB, :256] = total
                else:
                    acc[: 10 * SUB, low : low + 64] += total[:, :64]
                    acc[: 10 * SUB, low + 64 : low + 256] = total[:, 64:]
            for m in range(10):
                g1[step, 2 * m + parity + 1] = (acc[m * SUB : (m + 1) * SUB, :640] * s1[parity, m]).astype(BF16)

    def weight_step(step):
        for half in range(2):
            for group in range(3):
                lanes = 192 if group == 2 else 224
                part = tall(g1[step, 1:21, :, 224 * group : 224 * group + lanes])
                pixels = tall(x[half : half + 20, :, 512 * group : 512 * group + 512])
                acc1[half, :lanes] += dot(part, pixels, TN)
        for ky in range(4):
            total = None
            for group in range(3):
                part = tall(a1[ky % 2, ky // 2 : ky // 2 + 9, :, 192 * group : 192 * group + 256])
                term = dot(part, tall(pad2[1:10, :, 192 * group : 192 * group + 192]), TN)
                total = term if total is None else total + term
            acc2[ky] += total
        for ky in range(3):
            acc3[ky] += sum(
                dot(tall(a2[ky : ky + 7, :, 128 * pair : 128 * pair + 256]), tall(pad3[2:9, :, 128 * pair : 128 * pair + 128]), TN)
                for pair in range(4)
            )
        for at, (count, lanes) in enumerate(((20, 640), (9, 576), (7, 448))):
            part = jnp.zeros((8, lanes), F32)
            for y in range(count):
                piece = (g1[step, y + 1] if at == 0 else pad2[y + 1] if at == 1 else pad3[y + 2, :, :448]).astype(F32)
                for q in range(SUB // 8):
                    part += piece[8 * q : 8 * q + 8]
            bias_sums[at, :, :lanes] += part

    def one_step(step, _):
        slot = step % 2
        for c in raw_copies(step, slot):
            c.wait()

        @pl.when(step + 1 < steps)
        def _():
            for c in raw_copies(step + 1, 1 - slot):
                c.start()

        slope4 = forward(step, slot)

        @pl.when(role == 1)
        def _():
            probs_copy(step).start()

        @pl.when(online)
        def _():
            probs_copy(step).wait_recv()
            backward(step, slope4)
            @pl.when(step + 1 < steps)
            def _():
                grad_copy(step).start()

            weight_step(step)

        return 0

    lax.fori_loop(0, steps, one_step, 0)

    @pl.when(online)
    def _():
        flat = raw.reshape(2 * (TILES - 1) * SUB * STACK, 128)
        for y in range(7):
            block = dot(a3[y], g4[...], TN)
            for px in range(7):
                for q in range(4):
                    flat[pl.ds(3136 * q + 7 * y + px, 64, stride=49), :] = block[
                        64 * px : 64 * px + 64, 128 * q : 128 * q + 128
                    ]
        for q in range(4):
            send[:3136, 128 * q : 128 * q + 128] = flat[3136 * q : 3136 * q + 3136].astype(BF16)
        send[ROW_HEAD + 912 : ROW_TWO] = jnp.zeros((16, 512), BF16)
        head = dot(delta_all[...], a4[...], TN)
        send[ROW_HEAD : ROW_HEAD + 912] = head[:912].astype(BF16)
        send[ROW_HEAD + 912 : ROW_TWO] = jnp.concatenate([head[912:LOGITS], jnp.zeros((16 + 912 - LOGITS, 512), F32)], axis=0).astype(BF16)
        total = jnp.zeros((32, 256), F32)
        for half in range(2):
            folded = acc1[half, 0:32]
            for px in range(1, 7):
                folded += pltpu.roll(acc1[half, 32 * px : 32 * px + 32], 512 - 4 * px, 1)
            column = iota((512, 256), 1)
            goal = (column >> 6) * 128 + ((column >> 3) & 3) * 32 + (column & 7)
            mine = ((column >> 5) & 1) == half
            pick = onehot(mine & (iota((512, 256), 0) == goal), F32)
            total += dot(folded, pick, precision=HIGHEST)
        send[ROW_ONE:ROW_BIAS] = jnp.concatenate([total, jnp.zeros((32, 256), F32)], axis=1).astype(BF16)
        pieces = []
        for ky in range(4):
            for kx in range(4):
                pieces.append(
                    sum(acc2[ky, (2 * px + kx) * 32 : (2 * px + kx + 1) * 32, 64 * px : 64 * px + 64] for px in range(3))
                )
        pick = onehot(iota((512, 512), 1) == (iota((512, 512), 0) & 31) * 16 + (iota((512, 512), 0) >> 5), F32)
        send[ROW_TWO:ROW_THREE] = dot(jnp.concatenate(pieces, axis=0), pick, TN, HIGHEST).astype(BF16)
        pieces = []
        for ky in range(3):
            for kx in range(3):
                pieces.append(
                    sum(acc3[ky, (px + kx) * 64 : (px + kx + 1) * 64, 64 * px : 64 * px + 64] for px in range(2))
                )
        pick = onehot(iota((576, 576), 1) == (iota((576, 576), 0) & 63) * 9 + (iota((576, 576), 0) >> 6), F32)
        third = dot(jnp.concatenate(pieces, axis=0), pick, TN, HIGHEST)
        send[ROW_THREE:ROW_THREE_REST] = third[:, :512].astype(BF16)
        send[ROW_THREE_REST:ROW_ONE] = jnp.concatenate([third[:, 512:], jnp.zeros((64, 448), F32)], axis=1).astype(BF16)
        bias_rows = []
        for at, (size, copies) in enumerate(((32, 20), (64, 9), (64, 7))):
            fold = onehot((iota((size * copies, 512), 0) & (size - 1)) == iota((size * copies, 512), 1), F32)
            line = jnp.sum(bias_sums[at, :, : size * copies], axis=0, keepdims=True)
            bias_rows.append(dot(line, fold, precision=HIGHEST))
        bias_rows.append(jnp.sum(g4[...].astype(F32), axis=0, keepdims=True))
        head_bias = jnp.sum(delta_all[...].astype(F32), axis=0, keepdims=True)
        bias_rows.append(head_bias[:, :512])
        bias_rows.append(jnp.concatenate([head_bias[:, 512:], jnp.zeros((1, 1024 - LOGITS), F32)], axis=1))
        bias_rows.append(jnp.zeros((10, 512), F32))
        send[ROW_BIAS:ROW_LOSS] = jnp.concatenate(bias_rows, axis=0).astype(BF16)
        send[ROW_LOSS : ROW_LOSS + plan.loss_rows] = loss_sums[...].astype(BF16)
        if plan.rows > ROW_LOSS + plan.loss_rows:
            left = plan.rows - ROW_LOSS - plan.loss_rows
            send[ROW_LOSS + plan.loss_rows :] = jnp.zeros((left, 512), BF16)

    def stage_rows(stream, stage):
        base, size, order = plan.streams[stream]
        low = base
        for bit in order[:stage]:
            size //= 2
            low = low + bit_of(bit) * size
        return low, size

    def aligned(at):
        return pl.multiple_of(at, 16)

    def scatter_copy(stream, stage):
        base, size, order = plan.streams[stream]
        low, count = stage_rows(stream, stage)
        half = count // 2
        away = aligned(low + (1 - bit_of(order[stage])) * half)
        into = base + size - count
        index = stream * plan.bits + stage
        return remote(
            send.at[pl.ds(away, half)], landed.at[pl.ds(into, half)], rs_send.at[index], rs_recv.at[index],
            across(order[stage]),
        )

    def scatter_start(stage):
        for stream in range(len(plan.streams)):
            scatter_copy(stream, stage).start()

    def scatter_finish(stage):
        for stream, (base, size, order) in enumerate(plan.streams):
            scatter_copy(stream, stage).wait_recv()
            low, count = stage_rows(stream, stage)
            half = count // 2
            keep = aligned(low + bit_of(order[stage]) * half)
            into = base + size - count
            target = final if stage == plan.bits - 1 else send
            block = 64 if half % 64 == 0 else 16

            def add(i, _, keep=keep, into=into, target=target, block=block):
                at = aligned(keep + i * block)
                new = landed[pl.ds(aligned(into + i * block), block)].astype(F32)
                target[pl.ds(at, block)] = (send[pl.ds(at, block)].astype(F32) + new).astype(BF16)
                return 0

            lax.fori_loop(0, half // block, add, 0)
            if stage + 1 < plan.bits:
                scatter_copy(stream, stage + 1).start()
            else:
                over_copy(stream).start()
                gather_copy(stream, 0).start()
        if stage == plan.bits - 1:
            grad_copy(steps - 1).start()

    def over_copy(stream):
        low, count = stage_rows(stream, plan.bits)
        spot = pl.ds(aligned(low), count)
        return remote(final.at[spot], final.at[spot], x_send.at[stream], x_recv.at[stream], other_role)

    def gather_copy(stream, stage):
        order = plan.streams[stream][2]
        low, count = stage_rows(stream, plan.bits - stage)
        spot = pl.ds(aligned(low), count)
        index = stream * plan.bits + stage
        return remote(
            final.at[spot], final.at[spot], ag_send.at[index], ag_recv.at[index], across(order[plan.bits - 1 - stage])
        )

    def over_finish():
        for stream in range(len(plan.streams)):
            over_copy(stream).wait_recv()
            gather_copy(stream, 0).start()

    def gather_finish(stage):
        for stream in range(len(plan.streams)):
            gather_copy(stream, stage).wait_recv()
            if stage + 1 < plan.bits:
                gather_copy(stream, stage + 1).start()

    tile_rows = raw.reshape(2 * (TILES - 1) * SUB * STACK, 128)

    tile_pairs = raw.reshape((TILES - 1) * SUB * STACK, 2, 128)

    def tile_copies(step):
        return [
            pltpu.make_async_copy(
                tile_pairs.at[pl.ds(t * SUB, SUB)],
                frame_out.at[pl.ds(step * SUB, SUB), :, pl.ds(128 * t, 128)],
                tile_sem,
            )
            for t in range(TILES)
        ]

    def frame_step(step):
        acc[...] = dot(tall(g1[step, 1:22]), band_k[0], NT) + dot(tall(g1[step, 0:21]), band_k[1], NT)

        @pl.when(step > 0)
        def _():
            for c in tile_copies(step - 1):
                c.wait()

        for c in range(2):
            for t in range(TILES):
                pieces, at, end = [], 128 * t, min(128 * t + 128, PIX)
                while at < end:
                    band, inner = divmod(at, BAND)
                    size = min(end - at, BAND - inner)
                    pieces.append(acc[band * SUB : (band + 1) * SUB, WIDE * c + inner : WIDE * c + inner + size])
                    at += size
                if end < 128 * t + 128:
                    pieces.append(jnp.zeros((SUB, 128 * t + 128 - end), F32))
                tile_rows[pl.ds(t * SUB * 2 + c, SUB, stride=2), :] = (
                    pieces[0] if len(pieces) == 1 else jnp.concatenate(pieces, axis=1)
                )
        for c in tile_copies(step):
            c.start()

    @pl.when(online)
    def _():
        scatter_start(0)
        build_frame(k1_ref[:, 0:128], band_k)
        scatter_finish(0)

    @pl.when(role == 1)
    def _():
        kernel_copy.wait_recv()
        build_frame(k1_online[:, 128:256], band_k)

    def frame_and_more(step, _):
        @pl.when(role == 1)
        def _():
            grad_copy(step).wait_recv()

        frame_step(step)

        for stage in range(1, plan.bits):

            @pl.when(online & (step == min(3 * stage, steps - 1)))
            def _(stage=stage):
                scatter_finish(stage)

        @pl.when((role == 1) & (step == max(steps - 2, 0)))
        def _():
            over_finish()
            for stage in range(plan.bits - 1):
                gather_finish(stage)

        return 0

    lax.fori_loop(0, steps, frame_and_more, 0)

    @pl.when(online)
    def _():
        for stage in range(plan.bits - 1):
            gather_finish(stage)

    gather_finish(plan.bits - 1)
    out_copies = [
        pltpu.make_async_copy(final.at[pl.ds(0, ROW_HEAD)], dense_out, out_sem.at[0]),
        pltpu.make_async_copy(final.at[pl.ds(ROW_HEAD, plan.rows - ROW_HEAD)], sums_out, out_sem.at[1]),
    ]
    for c in out_copies:
        c.start()

    for c in tile_copies(steps - 1):
        c.wait()
    for stream in range(len(plan.streams)):
        for stage in range(plan.bits):
            gather_copy(stream, stage).wait_send()

    @pl.when(online)
    def _():
        kernel_copy.wait_send()
        for stream in range(len(plan.streams)):
            over_copy(stream).wait_send()
            for stage in range(plan.bits):
                scatter_copy(stream, stage).wait_send()

        def sent(step, _):
            grad_copy(step).wait_send()
            return 0

        lax.fori_loop(0, steps, sent, 0)

    @pl.when(role == 1)
    def _():
        def sent(step, _):
            probs_copy(step).wait_send()
            return 0

        lax.fori_loop(0, steps, sent, 0)

    for c in out_copies:
        c.wait()


def core(plan, frames, edge, weights, cols, tables):
    rows = frames.shape[1]
    steps = rows // SUB
    k1, k2, k3, w4, b1, b2, b3, b4, w5, b5 = weights
    vmem, hbm = pl.BlockSpec(memory_space=pltpu.VMEM), pl.BlockSpec(memory_space=pl.ANY)
    dma = pltpu.SemaphoreType.DMA
    streams = len(plan.streams)
    scratch = [
        pltpu.VMEM((2, TILES - 1, SUB, STACK, 128), F32),
        pltpu.VMEM((3 * STACK * SUB, 512), BF16),
        pltpu.VMEM((21, SUB, 1536), BF16),
        pltpu.VMEM((2, 10, SUB, 640), BF16),
        pltpu.VMEM((2, 10, SUB, 640), F32),
        pltpu.VMEM((9, SUB, 640), BF16),
        pltpu.VMEM((9, SUB, 576), F32),
        pltpu.VMEM((7, rows, 448), BF16),
        pltpu.VMEM((7, SUB, 448), F32),
        pltpu.VMEM((rows, 512), BF16),
        pltpu.VMEM((rows, 512), BF16),
        pltpu.VMEM((rows, LOGITS), BF16),
        pltpu.VMEM((steps, 22, SUB, 640), BF16),
        pltpu.VMEM((11, SUB, 576), BF16),
        pltpu.VMEM((11, SUB, 512), BF16),
        pltpu.VMEM((21 * SUB, 2 * WIDE), F32),
        pltpu.VMEM((2, 2 * WIDE, 640), BF16),
        pltpu.VMEM((2, 512, 224), BF16),
        pltpu.VMEM((1024, 192), BF16),
        pltpu.VMEM((768, 128), BF16),
        pltpu.VMEM((256, 384), BF16),
        pltpu.VMEM((3136, 512), BF16),
        pltpu.VMEM((8, 640), F32),
        pltpu.VMEM((2, 224, 512), F32),
        pltpu.VMEM((4, 256, 192), F32),
        pltpu.VMEM((3, 256, 128), F32),
        pltpu.VMEM((3, 8, 640), F32),
        pltpu.VMEM((plan.loss_rows, 512), F32),
        pltpu.VMEM((plan.rows, 512), BF16),
        pltpu.VMEM((plan.rows, 512), BF16),
        pltpu.VMEM((plan.rows, 512), BF16),
        pltpu.VMEM((steps, SUB, 128), F32),
        pltpu.VMEM((SUB, 128), F32),
        pltpu.VMEM((steps, SUB, 128), F32),
        pltpu.VMEM((plan.bits + 1, 8, 128), F32),
        pltpu.VMEM((plan.bits, 8, 128), F32),
        pltpu.VMEM((32, 256), BF16),
        dma((2,)), dma, dma, dma((steps,)), dma((steps,)), dma((steps,)), dma((steps,)),
        dma((plan.bits,)), dma((plan.bits,)), dma, dma,
        dma((streams * plan.bits,)), dma((streams * plan.bits,)), dma((streams * plan.bits,)), dma((streams * plan.bits,)),
        dma((streams,)), dma((streams,)), dma((2,)),
    ]
    return pl.pallas_call(
        functools.partial(core_kernel, plan, steps),
        in_specs=[hbm, vmem, vmem, vmem, vmem, hbm] + [vmem] * 9,
        out_specs=[hbm, hbm, hbm],
        out_shape=[
            jax.ShapeDtypeStruct((rows, 2, TILES * 128), F32),
            jax.ShapeDtypeStruct((ROW_HEAD, 512), BF16),
            jax.ShapeDtypeStruct((plan.rows - ROW_HEAD, 512), BF16),
        ],
        scratch_shapes=scratch,
        compiler_params=pltpu.CompilerParams(vmem_limit_bytes=63 << 20, collective_id=0, has_side_effects=True),
        name="core",
    )(frames, edge, k1, k2, k3, w4, b1, b2, b3, b4, w5, b5, cols, *tables)


def finish_kernel(frames, dense, sums, frame_out, w4, k1, b1, k2, b2, k3, b3, b4, w5, b5, losses):
    frame_out[...] = frames[:, :, :PIX]
    w4[...] = dense[...].astype(F32)

    def part(low, high):
        return sums[low - ROW_HEAD : high - ROW_HEAD]

    @pl.when(pl.program_id(0) == 0)
    def _():
        w5[:912] = part(ROW_HEAD, ROW_HEAD + 912).astype(F32)
        w5[912:] = part(ROW_HEAD + 912, ROW_TWO).astype(F32)[: LOGITS - 912]
        k2[...] = part(ROW_TWO, ROW_THREE).astype(F32)
        k3[:, :512] = part(ROW_THREE, ROW_THREE_REST).astype(F32)
        k3[:, 512:] = part(ROW_THREE_REST, ROW_ONE)[:, :64].astype(F32)
        k1[...] = part(ROW_ONE, ROW_BIAS)[:, :256].astype(F32)
        rows = part(ROW_BIAS, ROW_LOSS).astype(F32)
        b1[...] = rows[0:1, :32]
        b2[...] = rows[1:2, :64]
        b3[...] = rows[2:3, :64]
        b4[...] = rows[3:4]
        b5[:, :512] = rows[4:5]
        b5[:, 512:] = rows[5:6, : LOGITS - 512]
        losses[...] = part(ROW_LOSS, ROW_LOSS + losses.shape[0]).astype(F32)


def finish(plan, frames, dense, sums):
    rows = frames.shape[0]
    steps = rows // SUB
    small = ((32, 256), (1, 32), (64, 512), (1, 64), (64, 576), (1, 64), (1, 512), (LOGITS, 512), (1, LOGITS), (plan.loss_rows, 512))
    fixed = [pl.BlockSpec(s, lambda i: (0, 0)) for s in small]
    return pl.pallas_call(
        finish_kernel,
        grid=(steps,),
        in_specs=[
            pl.BlockSpec((SUB, 2, TILES * 128), lambda i: (i, 0, 0)),
            pl.BlockSpec((ROW_HEAD // 7, 512), lambda i: (jnp.minimum(i, 6), 0)),
            pl.BlockSpec(sums.shape, lambda i: (0, 0)),
        ],
        out_specs=[
            pl.BlockSpec((SUB, 2, PIX), lambda i: (i, 0, 0)),
            pl.BlockSpec((ROW_HEAD // 7, 512), lambda i: (jnp.minimum(i, 6), 0)),
            *fixed,
        ],
        out_shape=[jax.ShapeDtypeStruct(s, F32) for s in ((rows, 2, PIX), (ROW_HEAD, 512), *small)],
        compiler_params=pltpu.CompilerParams(vmem_limit_bytes=48 << 20),
        name="finish",
    )(frames, dense, sums)


def on_device(
    frames,
    conv1_weight,
    conv1_bias,
    conv2_weight,
    conv2_bias,
    conv3_weight,
    conv3_bias,
    dense_weight,
    dense_bias,
    head_weight,
    head_bias,
    taken_actions,
    next_actions,
    rewards,
    discounts,
    importance,
    buffer_slots,
):
    role, place = lax.axis_index("role"), lax.axis_index("batch")
    roles, batch = lax.axis_size("role"), lax.axis_size("batch")
    rows = frames.shape[1]
    slots = rows * batch
    plan = Plan(batch, slots)

    lane_action = jnp.asarray(np.arange(LOGITS)[None] // ATOMS, F32)
    compact = jnp.asarray(np.arange(128)[:, None] == np.arange(LOGITS)[None] % ATOMS, BF16)
    selected = jnp.where(role == 0, taken_actions, next_actions)
    columns = [rewards, discounts, importance, selected, taken_actions, buffer_slots // 512, buffer_slots % 512, rewards]
    cols = jnp.stack([c.astype(F32) for c in columns], axis=1)
    last = PIX - 128 * (TILES - 1)
    edge = jnp.pad(frames[0, :, :, PIX - last :].reshape(rows * STACK, last), ((0, 0), (0, 128 - last)))
    weights = (
        conv1_weight[0].T, conv2_weight[0].T, conv3_weight[0].T, dense_weight[0],
        conv1_bias, conv2_bias, conv3_bias, dense_bias, head_weight[0].T, head_bias,
    )
    wide_frames, dense, sums = core(plan, frames, edge, weights, cols, (lane_action, compact))
    frame_part, w4, k1, b1, k2, b2, k3, b3, b4, w5, b5, losses = finish(plan, wide_frames, dense, sums)
    own = slots // (roles * batch)
    priorities = lax.dynamic_slice_in_dim(losses.reshape(-1), (role * batch + place) * own, own, 0)
    return (frame_part, k1.T, b1[0], k2.T, b2[0], k3.T, b3[0], w4, b4[0], w5.T, b5[0], priorities)


def solution(mesh):
    in_specs = (
        P("role", "batch", None, None),
        P("role", None, None),
        P("role", None),
        P("role", None, None),
        P("role", None),
        P("role", None, None),
        P("role", None),
        P("role", None, None),
        P("role", None),
        P("role", None, None),
        P("role", None),
        P("batch"),
        P("batch"),
        P("batch"),
        P("batch"),
        P("batch"),
        P("batch"),
    )
    out_specs = (
        P("batch", "role", None),
        P(),
        P(),
        P(),
        P(),
        P(),
        P(),
        P(),
        P(),
        P(),
        P(),
        P(("role", "batch")),
    )
    return jax.shard_map(on_device, mesh=mesh, in_specs=in_specs, out_specs=out_specs, check_vma=False)
```

time: 628 us -> 206 us (0.33)
  waiting for transfers between devices: 215 us -> 0 us
  Pallas kernels: 0 us -> 196 us
  matrix products: 195 us -> 0 us
  local copies, waits for them, and re-layouts: 91.4 us -> 7.19 us
  blocking collectives: 69.7 us -> 0 us
  other arithmetic: 24.6 us -> 1.45 us
  between operations: 14.7 us -> 0.69 us
  starting transfers between devices: 7.68 us -> 0 us
    ppermute x5 -> x0, waiting for transfers between devices: 215 us -> none  [shifted_2(): return lax.ppermute(array, axis, pairs)]
    pallas_call x0 -> x2, Pallas kernels: none -> 196 us  [the longest x1 182 us: core(): pl.pallas_call(functools.partial(core_kernel, plan, steps), in_specs=[hbm...]
    conv_general_dilated x4 -> x0, matrix products: 189 us -> none  [the longest x1 154 us: conv_input_grad(): lax.conv_general_dilated(upstream, shaped, (1, 1), border, lhs_dilation=(...]
    psum x2 -> x0, blocking collectives: 69.7 us -> none  [the longest x1 48.4 us: on_device(): lax.psum((one_wg, one_bg, two_wg, two_bg, three_wg, three_bg, dense_wg, d...]
    unnamed x48 -> x5, local copies, waits for them, and re-layouts: 40.7 us -> 3.2 us
    convert_element_type x2 -> x0, local copies, waits for them, and re-layouts: 30.9 us -> none  [the longest x1 30 us: on_device(): pixels = frames[0].astype(jnp.bfloat16).reshape(rows, STACK, SIDE, SIDE)]
    convert_element_type x3 -> x2, other arithmetic: 14 us -> 1.45 us  [on_device(): cols = jnp.stack([c.astype(F32) for c in columns], axis=1)]
    another operation x12 -> x2, local copies, waits for them, and re-layouts: 11.5 us -> 1.55 us  [on_device(): cols = jnp.stack([c.astype(F32) for c in columns], axis=1)]
  transfers between devices with their start and end apart: 6 -> 0, of which waited for: 1 -> 0; matrix products, arithmetic and copies ran while one was open for 32% -> 0% of each run, Pallas kernels for 0% -> 0%
where the time goes in v1:
time: 206 us; the launch traced here: 205 us
  Pallas kernels  196 us (95%)
  local copies, waits for them, and re-layouts  7.19 us (3%)
    pallas_call x1, Pallas kernels, core(): pl.pallas_call(functools.partial(core_kernel, plan, steps), in_specs=[hbm...  182 us
    pallas_call x1, Pallas kernels, finish(): pl.pallas_call(finish_kernel, grid=(steps,), in_specs=[pl.BlockSpec((SUB,...  13.8 us

profile of v1, /device:TPU:14, one launch (start us, length us, event | category | flops | bytes accessed | tf_op | source)
XLA Modules:
  0.0 205.1 jit_solution(3635732207334896865)
XLA Ops:
  0.7 0.8 fusion.2
  1.4 0.7 fusion
  2.1 0.8 stack.32
  2.9 0.8 copy.39.refs_12_
  3.7 1.0 slice.3
  4.7 0.8 pad.4.refs_1_
  5.5 182.0 %core.1 = (f32[224,2,7168]{2,1,0:T(2,128)}, bf16[3136,512]{1,0:T(8,128)(2,1)}, bf16[1216,512]{1,0:T(8,128)(2,1)}) custom-call(f32[1,224,4,7056]{3,2,1,0:T(4,128)} %refs_0_.1, f32[896,128]{1,0:T(8,128)} %pad.4.refs_1_, bf16[32,256]{1,0:T(8,128)(2,1)} %bitcast.39, bf16[64,512]{1,0:T(8,128)(2,1)} %bitcast.37, bf16[64,576]{1,0:T(8,128)(2,1)} %bitcast.36, ...), custom_call_target="tpu_custom_call" | custom-call | tf_op jit(solution)/shard_map/core/pallas_call | solution.py:747
  187.5 0.0 copy-start
  187.5 1.9 copy-done
  189.4 0.0 copy-start.1
  189.4 1.3 copy-done.1
  190.7 13.8 %finish.1 = (f32[224,2,7056]{2,1,0:T(2,128)}, f32[3136,512]{1,0:T(8,128)}, f32[32,256]{1,0:T(8,128)}, f32[1,32]{1,0:T(1,128)}, f32[64,512]{1,0:T(8,128)}, /*inde...) custom-call(f32[224,2,7168]{2,1,0:T(2,128)} %get-tuple-element.27.fr, ...), custom_call_target="tpu_custom_call" | custom-call | tf_op jit(solution)/shard_map/finish/pallas_call | solution.py:792
  204.5 0.6 dynamic_slice.3
  (1 shorter events, 0.0 us)
Async XLA Ops:
  187.5 1.9 copy-start
  189.4 1.3 copy-start.1

commit v2 on v1

--- a/solution.py
+++ b/solution.py
@@ -28,7 +28,8 @@
 TN = (((0,), (0,)), ((), ()))
 
 ROW_HEAD = 3136
-ROW_TWO = ROW_HEAD + 928
+ROW_REST = 4096
+ROW_TWO = 0
 ROW_THREE = ROW_TWO + 64
 ROW_THREE_REST = ROW_THREE + 64
 ROW_ONE = ROW_THREE_REST + 64
@@ -66,8 +67,10 @@
             raise ValueError("batch axis")
         self.loss_rows = -(-slots // (512 * 16)) * 16
         unit = 16 * batch
-        units = -(-(ROW_LOSS + self.loss_rows) // unit)
-        self.rows = units * unit
+        units = -(-ROW_REST // unit)
+        self.rest = units * unit
+        rest_units = -(-(ROW_LOSS + self.loss_rows) // unit)
+        self.rows = (units + rest_units) * unit
         count = min(4, units)
         up = list(range(self.bits))
         round_way = up[:1] + up[2:] + up[1:2]
@@ -76,6 +79,9 @@
             size = (units // count + (1 if s < units % count else 0)) * unit
             self.streams.append((at, size, up if s % 2 == 0 else round_way))
             at += size
+        self.first = list(range(count))
+        self.second = [count]
+        self.streams.append((at, rest_units * unit, up))
 
 
 def banded_first(kernel_t, channel, line, column, real, channels, lanes):
@@ -99,7 +105,7 @@
     row = iota((512, 1), 0)
     found = banded_first(kernel_t, row >> 7, (row >> 5) & 3, row & 31, row >= 0, STACK, 224)
     for half in range(2):
-        out[half] = found[half]
+        out[512 * half : 512 * half + 512] = found[half]
 
 
 def build_frame(kernel_t, out):
@@ -147,16 +153,35 @@
         out[512 * kind : 512 * kind + 512, :WIDE] = onehot(row == goal + (BAND * kind) % 128, BF16)
 
 
+def frame_products(grads, band_k, acc):
+    acc[...] = dot(tall(grads[1:22]), band_k[0], NT) + dot(tall(grads[0:21]), band_k[1], NT)
+
+
+def frame_tile(acc, c, t):
+    pieces, at, end = [], 128 * t, min(128 * t + 128, PIX)
+    while at < end:
+        band, inner = divmod(at, BAND)
+        size = min(end - at, BAND - inner)
+        pieces.append(acc[band * SUB : (band + 1) * SUB, WIDE * c + inner : WIDE * c + inner + size])
+        at += size
+    if end < 128 * t + 128:
+        pieces.append(jnp.zeros((SUB, 128 * t + 128 - end), F32))
+    return pieces[0] if len(pieces) == 1 else jnp.concatenate(pieces, axis=1)
+
+
 def core_kernel(plan, steps, *refs):
-    (x_hbm, edge, k1_ref, k2_ref, k3_ref, w4_hbm, b1_ref, b2_ref, b3_ref, b4, w5, b5, cols, lane_action, compact) = refs[:15]
-    frame_out, dense_out, sums_out = refs[15:18]
+    (
+        x_hbm, edge, k1_ref, k2_ref, k3_ref, w4_hbm, b1_ref, b2_ref, b3_ref, b4, w5, b5, taken, following, rewards, discounts,
+        weighting, buffer_slots, lane_action, compact,
+    ) = refs[:20]
+    frame_out, dense_out, sums_out, x_kept, a1_kept, a2_kept, pad2_kept, pad3_kept = refs[20:28]
     (
         raw, lines, x, a1, s1, a2, s2, a3, s3, a4, g4, delta_all, g1, pad2, pad3, acc, band_k,
         k1, k2, k3, k3_wide, w4, bias, acc1, acc2, acc3, bias_sums, loss_sums, send, landed, final, probs_all, logp, nexts,
-        totals, totals_in, k1_online,
-        raw_sem, w4_sem, tile_sem, probs_send, probs_recv, g1_send, g1_recv, tot_send, tot_recv, k1_send, k1_recv,
+        totals, totals_in, k1_online, cols, slope4,
+        keep_sem, back_sem, raw_sem, w4_sem, tile_sem, probs_send, probs_recv, g1_send, g1_recv, tot_send, tot_recv, k1_send, k1_recv,
         rs_send, rs_recv, ag_send, ag_recv, x_send, x_recv, out_sem,
-    ) = refs[18:]
+    ) = refs[28:]
     role, place = lax.axis_index("role"), lax.axis_index("batch")
     online = role == 0
 
@@ -190,15 +215,16 @@
     for bit in range(plan.bits):
         pl.semaphore_signal(barrier, inc=1, device_id=across(bit), device_id_type=MESH)
     pl.semaphore_signal(barrier, inc=1, device_id=other_role, device_id_type=MESH)
-    pl.semaphore_wait(barrier, plan.bits + 1)
-
-    kernel_copy = remote(k1_ref, k1_online, k1_send, k1_recv, other_role)
-
-    @pl.when(online)
-    def _():
-        kernel_copy.start()
-
-    totals[0] = jnp.broadcast_to(jnp.sum(cols[:, 2:3], axis=0, keepdims=True), (8, 128))
+
+    slot_number = buffer_slots[...].astype(F32)
+    slot_row = jnp.floor(slot_number * (1.0 / 512))
+    taken_number = taken[...].astype(F32)
+    facts = [
+        rewards[...], discounts[...], weighting[...], jnp.where(online, taken_number, following[...].astype(F32)), taken_number,
+        slot_row, slot_number - 512.0 * slot_row, rewards[...],
+    ]
+    cols[...] = dot(jnp.concatenate(facts, axis=0), onehot(iota((8, 128), 0) == iota((8, 128), 1), F32), TN, HIGHEST)
+    totals[0] = jnp.broadcast_to(jnp.sum(weighting[...], axis=1, keepdims=True), (8, 128))
 
     def total_copy(stage):
         return remote(totals.at[stage], totals_in.at[stage], tot_send.at[stage], tot_recv.at[stage], across(stage))
@@ -210,31 +236,19 @@
         if stage < plan.bits:
             total_copy(stage).start()
 
-    todo = list(range(plan.bits + 1))
-    total_step(todo.pop(0))
     build_first(k1_ref[...], k1)
-    total_step(todo.pop(0))
     build_second(k2_ref[...], k2)
-    if len(todo) > 1:
-        total_step(todo.pop(0))
     build_third(k3_ref[...], k3, k3_wide)
-    if len(todo) > 1:
-        total_step(todo.pop(0))
-    bias[...] = jnp.zeros_like(bias)
-    for at, (ref, size, copies) in enumerate(((b1_ref, 32, 20), (b2_ref, 64, 9), (b3_ref, 64, 7))):
-        repeat = onehot((iota((size, size * copies), 1) & (size - 1)) == iota((size, size * copies), 0), F32)
-        bias[at : at + 1, : size * copies] = dot(ref[...], repeat, precision=HIGHEST)
-    acc1[...] = jnp.zeros_like(acc1)
-    acc2[...] = jnp.zeros_like(acc2)
-    acc3[...] = jnp.zeros_like(acc3)
-    bias_sums[...] = jnp.zeros_like(bias_sums)
-    loss_sums[...] = jnp.zeros_like(loss_sums)
-    pad3[...] = jnp.zeros_like(pad3)
-    pad2[...] = jnp.zeros_like(pad2)
-    a2[...] = jnp.zeros_like(a2)
-    for step in range(steps):
-        g1[step, 0] = jnp.zeros((SUB, 640), BF16)
-        g1[step, 21] = jnp.zeros((SUB, 640), BF16)
+
+    kernel_copy = remote(k1_ref, k1_online, k1_send, k1_recv, other_role)
+
+    pl.semaphore_wait(barrier, plan.bits + 1)
+    total_step(0)
+
+    @pl.when(online)
+    def _():
+        kernel_copy.start()
+
     weight_copy.wait()
     spare = raw.reshape(2, (TILES - 1) * SUB * STACK, 128)
     for pair in range(2):
@@ -247,15 +261,34 @@
                 w4[64 * spot : 64 * spot + 64, low : low + 128] = spare[
                     1, pl.ds(3136 * q + spot, 64, stride=49), :
                 ].astype(BF16)
+    total_step(1)
     build_picks(send)
-    while todo:
-        total_step(todo.pop(0))
-    for stage in range(plan.bits):
-        total_copy(stage).wait_send()
+    bias[...] = jnp.zeros_like(bias)
+    for at, (ref, size, copies) in enumerate(((b1_ref, 32, 20), (b2_ref, 64, 9), (b3_ref, 64, 7))):
+        repeat = onehot((iota((size, size * copies), 1) & (size - 1)) == iota((size, size * copies), 0), F32)
+        bias[at : at + 1, : size * copies] = dot(ref[...], repeat, precision=HIGHEST)
+    total_step(2)
+    acc1[...] = jnp.zeros_like(acc1)
+    acc2[...] = jnp.zeros_like(acc2)
+    acc3[...] = jnp.zeros_like(acc3)
+    bias_sums[...] = jnp.zeros_like(bias_sums)
+    loss_sums[...] = jnp.zeros_like(loss_sums)
+    pad3[...] = jnp.zeros_like(pad3)
+    pad2[...] = jnp.zeros_like(pad2)
+    a2[...] = jnp.zeros_like(a2)
+    for step in range(steps):
+        g1[step, 0] = jnp.zeros((SUB, 640), BF16)
+        g1[step, 21] = jnp.zeros((SUB, 640), BF16)
 
     raw_flat = raw.reshape(2, TILES - 1, SUB * STACK, 128)
 
-    def forward(step, slot):
+    def forward(step, slot, hooks=()):
+        hooks = list(hooks)
+
+        def hook():
+            if hooks:
+                hooks.pop(0)()
+
         rows = pl.ds(pl.multiple_of(step * SUB, SUB), SUB)
         own = cols[rows, :]
         for kind in range(8):
@@ -268,7 +301,8 @@
                         if low + t < TILES - 1:
                             piece = raw_flat[slot, low + t, pl.ds(c, SUB, stride=STACK), :]
                         else:
-                            piece = edge[pl.ds(step * (SUB * STACK) + c, SUB, stride=STACK), :]
+                            piece = edge[pl.ds(pl.multiple_of(step * SUB, SUB), SUB), c, :]
+                            piece = jnp.concatenate([piece, jnp.zeros((SUB, 128 - piece.shape[1]), F32)], axis=1)
                         lines[place_at : place_at + SUB, 128 * t : 128 * t + 128] = piece.astype(BF16)
             count = len(bands) * STACK * SUB
             sorted_lines = dot(lines[:count], send[512 * kind : 512 * kind + 512, :WIDE]).astype(BF16)
@@ -279,15 +313,17 @@
                         x[band, :, 512 * group + 128 * c : 512 * group + 128 * c + 128] = sorted_lines[
                             place_at : place_at + SUB, 128 * group : 128 * group + 128
                         ]
+        hook()
         for group, lanes in enumerate((224, 224, 192)):
             part = tall(x[:, :, 512 * group : 512 * group + 512])
-            acc[: 20 * SUB, 224 * group : 224 * group + lanes] = dot(part[: 20 * SUB], k1[0, :, :lanes]) + dot(
-                part[SUB:], k1[1, :, :lanes]
-            )
+            joined = jnp.concatenate([part[: 20 * SUB], part[SUB:]], axis=1)
+            acc[: 20 * SUB, 224 * group : 224 * group + lanes] = dot(joined, k1[:, :lanes])
+        hook()
         for y in range(20):
             act, slope = silu_and_slope(acc[y * SUB : (y + 1) * SUB, :640] + bias[0:1, :640])
             a1[y % 2, y // 2] = act
             s1[y % 2, y // 2] = slope
+        hook()
         for group in range(3):
             even, odd = (tall(a1[p, :, :, 192 * group : 192 * group + 256]) for p in range(2))
             joined = jnp.concatenate([even[: 9 * SUB], odd[: 9 * SUB], even[SUB:], odd[SUB:]], axis=1)
@@ -296,17 +332,19 @@
             act, slope = silu_and_slope(acc[y * SUB : (y + 1) * SUB, :576] + bias[1:2, :576])
             a2[y, :, :576] = act
             s2[y] = slope
+        hook()
         for pair in range(4):
             low = 128 * pair
             joined = jnp.concatenate([tall(a2[ky : ky + 7, :, low : low + 256]) for ky in range(3)], axis=1)
             acc[: 7 * SUB, low : low + 128] = dot(joined, k3[...])
+        hook()
         pre4 = b4[...]
         for y in range(7):
             act, slope = silu_and_slope(acc[y * SUB : (y + 1) * SUB, :448] + bias[2:3, :448])
             a3[y, rows, :] = act
             s3[y] = slope
             pre4 = pre4 + dot(act, w4[448 * y : 448 * y + 448])
-        act, slope4 = silu_and_slope(pre4)
+        act, slope = silu_and_slope(pre4)
         a4[rows, :] = act
         logits = dot(act, w5[...], NT) + b5[...]
         picked = jnp.where(lane_action[...] == own[:, 3:4], logits, 0.0)
@@ -322,15 +360,20 @@
         sums = jnp.sum(exps, axis=1, keepdims=True)
         probs_all[step] = exps / sums
         logp[...] = jnp.where(real, shifted - jnp.log(sums), 0.0)
-        return slope4
+        return slope
 
     def probs_copy(step):
         return remote(probs_all.at[step], nexts.at[step], probs_send.at[step], probs_recv.at[step], other_role)
 
-    def grad_copy(step):
-        return remote(g1.at[step, pl.ds(1, 20)], g1.at[step, pl.ds(1, 20)], g1_send.at[step], g1_recv.at[step], other_role)
-
-    def backward(step, slope4):
+    def grad_copy(step, half):
+        spot = g1.at[step, pl.ds(1 + 10 * half, 10)]
+        return remote(spot, spot, g1_send.at[2 * step + half], g1_recv.at[2 * step + half], other_role)
+
+    def grad_start(step):
+        for half in range(2):
+            grad_copy(step, half).start()
+
+    def backward(step):
         rows = pl.ds(pl.multiple_of(step * SUB, SUB), SUB)
         own = cols[rows, :]
         nodes = iota((SUB, 128), 1).astype(F32)
@@ -352,7 +395,7 @@
         spread = dot(delta, compact[...])
         delta_full = jnp.where(lane_action[...] == own[:, 4:5], spread, 0.0).astype(BF16)
         delta_all[rows, :] = delta_full
-        grad4 = (dot(delta_full, w5[...]) * slope4).astype(BF16)
+        grad4 = (dot(delta_full, w5[...]) * slope4[...]).astype(BF16)
         g4[rows, :] = grad4
         for y in range(7):
             pad3[y + 2, :, :448] = (dot(grad4, w4[448 * y : 448 * y + 448], NT) * s3[y]).astype(BF16)
@@ -382,25 +425,102 @@
             for m in range(10):
                 g1[step, 2 * m + parity + 1] = (acc[m * SUB : (m + 1) * SUB, :640] * s1[parity, m]).astype(BF16)
 
-    def weight_step(step):
-        for half in range(2):
-            for group in range(3):
-                lanes = 192 if group == 2 else 224
-                part = tall(g1[step, 1:21, :, 224 * group : 224 * group + lanes])
-                pixels = tall(x[half : half + 20, :, 512 * group : 512 * group + 512])
-                acc1[half, :lanes] += dot(part, pixels, TN)
-        for ky in range(4):
-            total = None
-            for group in range(3):
-                part = tall(a1[ky % 2, ky // 2 : ky // 2 + 9, :, 192 * group : 192 * group + 256])
-                term = dot(part, tall(pad2[1:10, :, 192 * group : 192 * group + 192]), TN)
-                total = term if total is None else total + term
-            acc2[ky] += total
-        for ky in range(3):
-            acc3[ky] += sum(
-                dot(tall(a2[ky : ky + 7, :, 128 * pair : 128 * pair + 256]), tall(pad3[2:9, :, 128 * pair : 128 * pair + 128]), TN)
-                for pair in range(4)
-            )
+    kept = ((x, x_kept), (a1, a1_kept), (a2, a2_kept), (pad2, pad2_kept), (pad3, pad3_kept))
+
+    def keep_copies(step, low, high):
+        return [pltpu.make_async_copy(kept[i][0], kept[i][1].at[step], keep_sem.at[i]) for i in range(low, high)]
+
+    def back_copies(step, low, high):
+        return [pltpu.make_async_copy(kept[i][1].at[step], kept[i][0], back_sem.at[i]) for i in range(low, high)]
+
+    early = max(steps - 3, 0)
+
+    def prefetch(step, slot):
+        @pl.when(step < steps)
+        def _():
+            for c in raw_copies(step, slot):
+                c.start()
+
+    def raw_wait(step, slot):
+        for c in raw_copies(step, slot):
+            c.wait()
+
+    def after_forward(step):
+        @pl.when(role == 1)
+        def _():
+            probs_copy(step).start()
+
+        @pl.when(online & (step + 1 < steps))
+        def _():
+            for c in keep_copies(step, 0, 3):
+                c.start()
+
+    raw_wait(0, 0)
+    prefetch(1, 1)
+    hooks = [functools.partial(total_step, stage) for stage in range(3, plan.bits + 1)]
+    slope4[...] = forward(0, 0, hooks[:6])
+    for late in hooks[6:]:
+        late()
+    after_forward(0)
+
+    def one_step(step, _):
+        @pl.when(online)
+        def _():
+            @pl.when(step > 0)
+            def _():
+                for c in keep_copies(step - 1, 3, 5):
+                    c.wait()
+
+            probs_copy(step).wait_recv()
+            backward(step)
+
+            @pl.when(step < early)
+            def _():
+                grad_start(step)
+
+            @pl.when(step + 1 < steps)
+            def _():
+                for c in keep_copies(step, 3, 5):
+                    c.start()
+
+        @pl.when(step + 1 < steps)
+        def _():
+            following_step = step + 1
+            slot = following_step % 2
+            raw_wait(following_step, slot)
+            prefetch(following_step + 1, 1 - slot)
+
+            @pl.when(online)
+            def _():
+                for c in keep_copies(step, 0, 3):
+                    c.wait()
+
+            slope4[...] = forward(following_step, slot)
+            after_forward(following_step)
+
+        return 0
+
+    lax.fori_loop(0, steps, one_step, 0)
+
+    for stage in range(plan.bits):
+        total_copy(stage).wait_send()
+
+    def late_layers(step):
+        total = None
+        for group in range(3):
+            low = 192 * group
+            even, odd = (tall(a1[p, :, :, low : low + 256]) for p in range(2))
+            joined = jnp.concatenate([even[: 9 * SUB], odd[: 9 * SUB], even[SUB:], odd[SUB:]], axis=1)
+            term = dot(tall(pad2[1:10, :, low : low + 192]), joined, TN)
+            total = term if total is None else total + term
+        acc2[...] += total
+        total = None
+        for pair in range(4):
+            low = 128 * pair
+            joined = jnp.concatenate([tall(a2[ky : ky + 7, :, low : low + 256]) for ky in range(3)], axis=1)
+            term = dot(tall(pad3[2:9, :, low : low + 128]), joined, TN)
+            total = term if total is None else total + term
+        acc3[...] += total
         for at, (count, lanes) in enumerate(((20, 640), (9, 576), (7, 448))):
             part = jnp.zeros((8, lanes), F32)
             for y in range(count):
@@ -409,38 +529,40 @@
                     part += piece[8 * q : 8 * q + 8]
             bias_sums[at, :, :lanes] += part
 
-    def one_step(step, _):
-        slot = step % 2
-        for c in raw_copies(step, slot):
-            c.wait()
-
-        @pl.when(step + 1 < steps)
-        def _():
-            for c in raw_copies(step + 1, 1 - slot):
+    def first_layer(step):
+        for group in range(3):
+            lanes = 192 if group == 2 else 224
+            part = tall(g1[step, 1:21, :, 224 * group : 224 * group + lanes])
+            pixels = tall(x[:, :, 512 * group : 512 * group + 512])
+            joined = jnp.concatenate([pixels[: 20 * SUB], pixels[SUB:]], axis=1)
+            acc1[:lanes] += dot(part, joined, TN)
+
+    def weight_step(turn, step):
+        @pl.when(turn > 0)
+        def _():
+            for c in back_copies(step, 1, 5):
+                c.wait()
+
+        late_layers(step)
+
+        @pl.when(turn + 1 < steps)
+        def _():
+            for c in back_copies(turn, 1, 5):
                 c.start()
 
-        slope4 = forward(step, slot)
-
-        @pl.when(role == 1)
-        def _():
-            probs_copy(step).start()
-
-        @pl.when(online)
-        def _():
-            probs_copy(step).wait_recv()
-            backward(step, slope4)
-            @pl.when(step + 1 < steps)
-            def _():
-                grad_copy(step).start()
-
-            weight_step(step)
-
-        return 0
-
-    lax.fori_loop(0, steps, one_step, 0)
-
-    @pl.when(online)
-    def _():
+        @pl.when(turn > 0)
+        def _():
+            for c in back_copies(step, 0, 1):
+                c.wait()
+
+        first_layer(step)
+
+        @pl.when(turn + 1 < steps)
+        def _():
+            for c in back_copies(turn, 0, 1):
+                c.start()
+
+    def dense_sums():
         flat = raw.reshape(2 * (TILES - 1) * SUB * STACK, 128)
         for y in range(7):
             block = dot(a3[y], g4[...], TN)
@@ -451,39 +573,38 @@
                     ]
         for q in range(4):
             send[:3136, 128 * q : 128 * q + 128] = flat[3136 * q : 3136 * q + 3136].astype(BF16)
-        send[ROW_HEAD + 912 : ROW_TWO] = jnp.zeros((16, 512), BF16)
         head = dot(delta_all[...], a4[...], TN)
         send[ROW_HEAD : ROW_HEAD + 912] = head[:912].astype(BF16)
-        send[ROW_HEAD + 912 : ROW_TWO] = jnp.concatenate([head[912:LOGITS], jnp.zeros((16 + 912 - LOGITS, 512), F32)], axis=0).astype(BF16)
-        total = jnp.zeros((32, 256), F32)
-        for half in range(2):
-            folded = acc1[half, 0:32]
-            for px in range(1, 7):
-                folded += pltpu.roll(acc1[half, 32 * px : 32 * px + 32], 512 - 4 * px, 1)
-            column = iota((512, 256), 1)
-            goal = (column >> 6) * 128 + ((column >> 3) & 3) * 32 + (column & 7)
-            mine = ((column >> 5) & 1) == half
-            pick = onehot(mine & (iota((512, 256), 0) == goal), F32)
-            total += dot(folded, pick, precision=HIGHEST)
-        send[ROW_ONE:ROW_BIAS] = jnp.concatenate([total, jnp.zeros((32, 256), F32)], axis=1).astype(BF16)
-        pieces = []
-        for ky in range(4):
-            for kx in range(4):
-                pieces.append(
-                    sum(acc2[ky, (2 * px + kx) * 32 : (2 * px + kx + 1) * 32, 64 * px : 64 * px + 64] for px in range(3))
-                )
-        pick = onehot(iota((512, 512), 1) == (iota((512, 512), 0) & 31) * 16 + (iota((512, 512), 0) >> 5), F32)
-        send[ROW_TWO:ROW_THREE] = dot(jnp.concatenate(pieces, axis=0), pick, TN, HIGHEST).astype(BF16)
-        pieces = []
-        for ky in range(3):
-            for kx in range(3):
-                pieces.append(
-                    sum(acc3[ky, (px + kx) * 64 : (px + kx + 1) * 64, 64 * px : 64 * px + 64] for px in range(2))
-                )
-        pick = onehot(iota((576, 576), 1) == (iota((576, 576), 0) & 63) * 9 + (iota((576, 576), 0) >> 6), F32)
-        third = dot(jnp.concatenate(pieces, axis=0), pick, TN, HIGHEST)
-        send[ROW_THREE:ROW_THREE_REST] = third[:, :512].astype(BF16)
-        send[ROW_THREE_REST:ROW_ONE] = jnp.concatenate([third[:, 512:], jnp.zeros((64, 448), F32)], axis=1).astype(BF16)
+        send[ROW_HEAD + 912 : ROW_HEAD + 928] = jnp.concatenate(
+            [head[912:LOGITS], jnp.zeros((928 - LOGITS, 512), F32)], axis=0
+        ).astype(BF16)
+        send[ROW_HEAD + 928 : plan.rest] = jnp.zeros((plan.rest - ROW_HEAD - 928, 512), BF16)
+
+    def other_sums():
+        def put(low, value):
+            send[plan.rest + low : plan.rest + low + value.shape[0]] = value.astype(BF16)
+
+        folded = acc1[0:32]
+        for px in range(1, 7):
+            folded += pltpu.roll(acc1[32 * px : 32 * px + 32], 1024 - 4 * px, 1)
+        column = iota((1024, 256), 1)
+        goal = ((column >> 5) & 1) * 512 + (column >> 6) * 128 + ((column >> 3) & 3) * 32 + (column & 7)
+        pick = onehot(iota((1024, 256), 0) == goal, F32)
+        put(ROW_ONE, jnp.concatenate([dot(folded, pick, precision=HIGHEST), jnp.zeros((32, 256), F32)], axis=1))
+        folded = acc2[0:64]
+        for px in range(1, 3):
+            folded += pltpu.roll(acc2[64 * px : 64 * px + 64], 1024 - 64 * px, 1)
+        column = iota((1024, 512), 1)
+        goal = ((column >> 2) & 3) * 256 + (column & 3) * 32 + (column >> 4)
+        pick = onehot(iota((1024, 512), 0) == goal, F32)
+        put(ROW_TWO, dot(folded, pick, precision=HIGHEST))
+        folded = acc3[0:64] + pltpu.roll(acc3[64:128], 768 - 64, 1)
+        row = iota((768, 576), 0)
+        goal = (row & 63) * 9 + (row >> 8) * 3 + ((row >> 6) & 3)
+        pick = onehot((iota((768, 576), 1) == goal) & (((row >> 6) & 3) < 3), F32)
+        third = dot(folded, pick, precision=HIGHEST)
+        put(ROW_THREE, third[:, :512])
+        put(ROW_THREE_REST, jnp.concatenate([third[:, 512:], jnp.zeros((64, 448), F32)], axis=1))
         bias_rows = []
         for at, (size, copies) in enumerate(((32, 20), (64, 9), (64, 7))):
             fold = onehot((iota((size * copies, 512), 0) & (size - 1)) == iota((size * copies, 512), 1), F32)
@@ -494,11 +615,11 @@
         bias_rows.append(head_bias[:, :512])
         bias_rows.append(jnp.concatenate([head_bias[:, 512:], jnp.zeros((1, 1024 - LOGITS), F32)], axis=1))
         bias_rows.append(jnp.zeros((10, 512), F32))
-        send[ROW_BIAS:ROW_LOSS] = jnp.concatenate(bias_rows, axis=0).astype(BF16)
-        send[ROW_LOSS : ROW_LOSS + plan.loss_rows] = loss_sums[...].astype(BF16)
-        if plan.rows > ROW_LOSS + plan.loss_rows:
-            left = plan.rows - ROW_LOSS - plan.loss_rows
-            send[ROW_LOSS + plan.loss_rows :] = jnp.zeros((left, 512), BF16)
+        put(ROW_BIAS, jnp.concatenate(bias_rows, axis=0))
+        put(ROW_LOSS, loss_sums[...])
+        left = plan.rows - plan.rest - ROW_LOSS - plan.loss_rows
+        if left:
+            put(ROW_LOSS + plan.loss_rows, jnp.zeros((left, 512), F32))
 
     def stage_rows(stream, stage):
         base, size, order = plan.streams[stream]
@@ -523,12 +644,13 @@
             across(order[stage]),
         )
 
-    def scatter_start(stage):
-        for stream in range(len(plan.streams)):
-            scatter_copy(stream, stage).start()
-
-    def scatter_finish(stage):
-        for stream, (base, size, order) in enumerate(plan.streams):
+    def scatter_start(streams):
+        for stream in streams:
+            scatter_copy(stream, 0).start()
+
+    def scatter_finish(stage, streams):
+        for stream in streams:
+            base, size, order = plan.streams[stream]
             scatter_copy(stream, stage).wait_recv()
             low, count = stage_rows(stream, stage)
             half = count // 2
@@ -549,8 +671,6 @@
             else:
                 over_copy(stream).start()
                 gather_copy(stream, 0).start()
-        if stage == plan.bits - 1:
-            grad_copy(steps - 1).start()
 
     def over_copy(stream):
         low, count = stage_rows(stream, plan.bits)
@@ -566,13 +686,13 @@
             final.at[spot], final.at[spot], ag_send.at[index], ag_recv.at[index], across(order[plan.bits - 1 - stage])
         )
 
-    def over_finish():
-        for stream in range(len(plan.streams)):
+    def over_finish(streams):
+        for stream in streams:
             over_copy(stream).wait_recv()
             gather_copy(stream, 0).start()
 
-    def gather_finish(stage):
-        for stream in range(len(plan.streams)):
+    def gather_finish(stage, streams):
+        for stream in streams:
             gather_copy(stream, stage).wait_recv()
             if stage + 1 < plan.bits:
                 gather_copy(stream, stage + 1).start()
@@ -592,7 +712,7 @@
         ]
 
     def frame_step(step):
-        acc[...] = dot(tall(g1[step, 1:22]), band_k[0], NT) + dot(tall(g1[step, 0:21]), band_k[1], NT)
+        frame_products(g1.at[step], band_k, acc)
 
         @pl.when(step > 0)
         def _():
@@ -601,25 +721,43 @@
 
         for c in range(2):
             for t in range(TILES):
-                pieces, at, end = [], 128 * t, min(128 * t + 128, PIX)
-                while at < end:
-                    band, inner = divmod(at, BAND)
-                    size = min(end - at, BAND - inner)
-                    pieces.append(acc[band * SUB : (band + 1) * SUB, WIDE * c + inner : WIDE * c + inner + size])
-                    at += size
-                if end < 128 * t + 128:
-                    pieces.append(jnp.zeros((SUB, 128 * t + 128 - end), F32))
-                tile_rows[pl.ds(t * SUB * 2 + c, SUB, stride=2), :] = (
-                    pieces[0] if len(pieces) == 1 else jnp.concatenate(pieces, axis=1)
-                )
+                tile_rows[pl.ds(t * SUB * 2 + c, SUB, stride=2), :] = frame_tile(acc, c, t)
         for c in tile_copies(step):
             c.start()
 
+    bits, first, second = plan.bits, plan.first, plan.second
+
+    late_grads = [(step, half) for step in range(early, steps) for half in range(2)]
+    issue = {"soon": late_grads[:-4], "mid": late_grads[-4:-3], "over": late_grads[-3:-2], "last": late_grads[-2:]}
+
+    def grads_at(moment):
+        for step, half in issue[moment]:
+            grad_copy(step, half).start()
+
+    def turn_at(number):
+        return min(number, steps - 1)
+
     @pl.when(online)
     def _():
-        scatter_start(0)
+        dense_sums()
+        scatter_start(first)
+
+        def turns(turn, _):
+            weight_step(turn, jnp.where(turn == 0, steps - 1, turn - 1))
+
+            @pl.when(turn == turn_at(1))
+            def _():
+                scatter_finish(0, first)
+                grads_at("soon")
+
+            return 0
+
+        lax.fori_loop(0, steps, turns, 0)
+        scatter_finish(1, first)
+        grads_at("mid")
+        other_sums()
+        scatter_start(second)
         build_frame(k1_ref[:, 0:128], band_k)
-        scatter_finish(0)
 
     @pl.when(role == 1)
     def _():
@@ -629,21 +767,48 @@
     def frame_and_more(step, _):
         @pl.when(role == 1)
         def _():
-            grad_copy(step).wait_recv()
+            for half in range(2):
+                grad_copy(step, half).wait_recv()
 
         frame_step(step)
 
-        for stage in range(1, plan.bits):
-
-            @pl.when(online & (step == min(3 * stage, steps - 1)))
-            def _(stage=stage):
-                scatter_finish(stage)
-
-        @pl.when((role == 1) & (step == max(steps - 2, 0)))
-        def _():
-            over_finish()
-            for stage in range(plan.bits - 1):
-                gather_finish(stage)
+        @pl.when(online & (step == 0))
+        def _():
+            scatter_finish(0, second)
+            scatter_finish(2, first)
+
+        @pl.when(online & (step == turn_at(1)))
+        def _():
+            scatter_finish(1, second)
+
+        @pl.when(online & (step == turn_at(2)))
+        def _():
+            for stage in range(3, bits):
+                scatter_finish(stage, first)
+            grads_at("over")
+            scatter_finish(2, second)
+
+        @pl.when(online & (step == turn_at(3)))
+        def _():
+            for stage in range(3, bits):
+                scatter_finish(stage, second)
+            grads_at("last")
+
+        @pl.when(online & (step == turn_at(5)))
+        def _():
+            gather_finish(0, first)
+            gather_finish(0, second)
+
+        @pl.when((role == 1) & (step == max(steps - 3, 0)))
+        def _():
+            over_finish(first)
+            for stage in range(bits):
+                gather_finish(stage, first)
+                if stage == 0:
+                    over_finish(second)
+                else:
+                    gather_finish(stage - 1, second)
+            gather_finish(bits - 1, second)
 
         return 0
 
@@ -651,10 +816,10 @@
 
     @pl.when(online)
     def _():
-        for stage in range(plan.bits - 1):
-            gather_finish(stage)
-
-    gather_finish(plan.bits - 1)
+        for stage in range(1, bits):
+            gather_finish(stage, first)
+            gather_finish(stage, second)
+
     out_copies = [
         pltpu.make_async_copy(final.at[pl.ds(0, ROW_HEAD)], dense_out, out_sem.at[0]),
         pltpu.make_async_copy(final.at[pl.ds(ROW_HEAD, plan.rows - ROW_HEAD)], sums_out, out_sem.at[1]),
@@ -677,7 +842,8 @@
                 scatter_copy(stream, stage).wait_send()
 
         def sent(step, _):
-            grad_copy(step).wait_send()
+            for half in range(2):
+                grad_copy(step, half).wait_send()
             return 0
 
         lax.fori_loop(0, steps, sent, 0)
@@ -694,7 +860,7 @@
         c.wait()
 
 
-def core(plan, frames, edge, weights, cols, tables):
+def core(plan, frames, edge, weights, facts, tables):
     rows = frames.shape[1]
     steps = rows // SUB
     k1, k2, k3, w4, b1, b2, b3, b4, w5, b5 = weights
@@ -719,15 +885,15 @@
         pltpu.VMEM((11, SUB, 512), BF16),
         pltpu.VMEM((21 * SUB, 2 * WIDE), F32),
         pltpu.VMEM((2, 2 * WIDE, 640), BF16),
-        pltpu.VMEM((2, 512, 224), BF16),
+        pltpu.VMEM((1024, 224), BF16),
         pltpu.VMEM((1024, 192), BF16),
         pltpu.VMEM((768, 128), BF16),
         pltpu.VMEM((256, 384), BF16),
         pltpu.VMEM((3136, 512), BF16),
         pltpu.VMEM((8, 640), F32),
-        pltpu.VMEM((2, 224, 512), F32),
-        pltpu.VMEM((4, 256, 192), F32),
-        pltpu.VMEM((3, 256, 128), F32),
+        pltpu.VMEM((224, 1024), F32),
+        pltpu.VMEM((192, 1024), F32),
+        pltpu.VMEM((128, 768), F32),
         pltpu.VMEM((3, 8, 640), F32),
         pltpu.VMEM((plan.loss_rows, 512), F32),
         pltpu.VMEM((plan.rows, 512), BF16),
@@ -739,37 +905,44 @@
         pltpu.VMEM((plan.bits + 1, 8, 128), F32),
         pltpu.VMEM((plan.bits, 8, 128), F32),
         pltpu.VMEM((32, 256), BF16),
-        dma((2,)), dma, dma, dma((steps,)), dma((steps,)), dma((steps,)), dma((steps,)),
+        pltpu.VMEM((rows, 128), F32),
+        pltpu.VMEM((SUB, 512), F32),
+        dma((5,)), dma((5,)), dma((2,)), dma, dma, dma((steps,)), dma((steps,)), dma((2 * steps,)), dma((2 * steps,)),
         dma((plan.bits,)), dma((plan.bits,)), dma, dma,
         dma((streams * plan.bits,)), dma((streams * plan.bits,)), dma((streams * plan.bits,)), dma((streams * plan.bits,)),
         dma((streams,)), dma((streams,)), dma((2,)),
     ]
     return pl.pallas_call(
         functools.partial(core_kernel, plan, steps),
-        in_specs=[hbm, vmem, vmem, vmem, vmem, hbm] + [vmem] * 9,
-        out_specs=[hbm, hbm, hbm],
+        in_specs=[hbm, vmem, vmem, vmem, vmem, hbm] + [vmem] * 14,
+        out_specs=[hbm] * 8,
         out_shape=[
             jax.ShapeDtypeStruct((rows, 2, TILES * 128), F32),
             jax.ShapeDtypeStruct((ROW_HEAD, 512), BF16),
             jax.ShapeDtypeStruct((plan.rows - ROW_HEAD, 512), BF16),
+            jax.ShapeDtypeStruct((steps - 1, 21, SUB, 1536), BF16),
+            jax.ShapeDtypeStruct((steps - 1, 2, 10, SUB, 640), BF16),
+            jax.ShapeDtypeStruct((steps - 1, 9, SUB, 640), BF16),
+            jax.ShapeDtypeStruct((steps - 1, 11, SUB, 576), BF16),
+            jax.ShapeDtypeStruct((steps - 1, 11, SUB, 512), BF16),
         ],
         scratch_shapes=scratch,
         compiler_params=pltpu.CompilerParams(vmem_limit_bytes=63 << 20, collective_id=0, has_side_effects=True),
         name="core",
-    )(frames, edge, k1, k2, k3, w4, b1, b2, b3, b4, w5, b5, cols, *tables)
-
-
-def finish_kernel(frames, dense, sums, frame_out, w4, k1, b1, k2, b2, k3, b3, b4, w5, b5, losses):
+    )(frames, edge, k1, k2, k3, w4, b1, b2, b3, b4, w5, b5, *facts, *tables)[:3]
+
+
+def finish_kernel(plan, own, frames, dense, sums, frame_out, w4, k1, b1, k2, b2, k3, b3, b4, w5, b5, losses):
     frame_out[...] = frames[:, :, :PIX]
     w4[...] = dense[...].astype(F32)
 
     def part(low, high):
-        return sums[low - ROW_HEAD : high - ROW_HEAD]
+        return sums[plan.rest - ROW_HEAD + low : plan.rest - ROW_HEAD + high]
 
     @pl.when(pl.program_id(0) == 0)
     def _():
-        w5[:912] = part(ROW_HEAD, ROW_HEAD + 912).astype(F32)
-        w5[912:] = part(ROW_HEAD + 912, ROW_TWO).astype(F32)[: LOGITS - 912]
+        w5[:912] = sums[:912].astype(F32)
+        w5[912:] = sums[912:928].astype(F32)[: LOGITS - 912]
         k2[...] = part(ROW_TWO, ROW_THREE).astype(F32)
         k3[:, :512] = part(ROW_THREE, ROW_THREE_REST).astype(F32)
         k3[:, 512:] = part(ROW_THREE_REST, ROW_ONE)[:, :64].astype(F32)
@@ -781,29 +954,33 @@
         b4[...] = rows[3:4]
         b5[:, :512] = rows[4:5]
         b5[:, 512:] = rows[5:6, : LOGITS - 512]
-        losses[...] = part(ROW_LOSS, ROW_LOSS + losses.shape[0]).astype(F32)
-
-
-def finish(plan, frames, dense, sums):
+        device = lax.axis_index("role") * plan.batch + lax.axis_index("batch")
+        slot = device * own + iota((1, own), 1)
+        chosen = dot(part(ROW_LOSS, ROW_LOSS + plan.loss_rows), onehot(iota((512, own), 0) == (slot & 511), BF16))
+        mine = iota((plan.loss_rows, own), 0) == (slot >> 9)
+        losses[...] = jnp.sum(jnp.where(mine, chosen, 0.0), axis=0, keepdims=True)
+
+
+def finish(plan, own, frames, dense, sums):
     rows = frames.shape[0]
-    steps = rows // SUB
-    small = ((32, 256), (1, 32), (64, 512), (1, 64), (64, 576), (1, 64), (1, 512), (LOGITS, 512), (1, LOGITS), (plan.loss_rows, 512))
-    fixed = [pl.BlockSpec(s, lambda i: (0, 0)) for s in small]
+    small = ((32, 256), (1, 32), (64, 512), (1, 64), (64, 576), (1, 64), (1, 512), (LOGITS, 512), (1, LOGITS), (1, own))
+    block, pieces = (56, 4) if rows % 56 == 0 else (16, 14)
+    frame_at, dense_at = (lambda i: (i, 0, 0)), (lambda i: (jnp.minimum(i, pieces - 1), 0))
     return pl.pallas_call(
-        finish_kernel,
-        grid=(steps,),
+        functools.partial(finish_kernel, plan, own),
+        grid=(rows // block,),
         in_specs=[
-            pl.BlockSpec((SUB, 2, TILES * 128), lambda i: (i, 0, 0)),
-            pl.BlockSpec((ROW_HEAD // 7, 512), lambda i: (jnp.minimum(i, 6), 0)),
+            pl.BlockSpec((block, 2, TILES * 128), frame_at),
+            pl.BlockSpec((ROW_HEAD // pieces, 512), dense_at),
             pl.BlockSpec(sums.shape, lambda i: (0, 0)),
         ],
         out_specs=[
-            pl.BlockSpec((SUB, 2, PIX), lambda i: (i, 0, 0)),
-            pl.BlockSpec((ROW_HEAD // 7, 512), lambda i: (jnp.minimum(i, 6), 0)),
-            *fixed,
+            pl.BlockSpec((block, 2, PIX), frame_at),
+            pl.BlockSpec((ROW_HEAD // pieces, 512), dense_at),
+            *[pl.BlockSpec(s, lambda i: (0, 0)) for s in small],
         ],
         out_shape=[jax.ShapeDtypeStruct(s, F32) for s in ((rows, 2, PIX), (ROW_HEAD, 512), *small)],
-        compiler_params=pltpu.CompilerParams(vmem_limit_bytes=48 << 20),
+        compiler_params=pltpu.CompilerParams(vmem_limit_bytes=60 << 20),
         name="finish",
     )(frames, dense, sums)
 
@@ -827,7 +1004,6 @@
     importance,
     buffer_slots,
 ):
-    role, place = lax.axis_index("role"), lax.axis_index("batch")
     roles, batch = lax.axis_size("role"), lax.axis_size("batch")
     rows = frames.shape[1]
     slots = rows * batch
@@ -835,20 +1011,17 @@
 
     lane_action = jnp.asarray(np.arange(LOGITS)[None] // ATOMS, F32)
     compact = jnp.asarray(np.arange(128)[:, None] == np.arange(LOGITS)[None] % ATOMS, BF16)
-    selected = jnp.where(role == 0, taken_actions, next_actions)
-    columns = [rewards, discounts, importance, selected, taken_actions, buffer_slots // 512, buffer_slots % 512, rewards]
-    cols = jnp.stack([c.astype(F32) for c in columns], axis=1)
-    last = PIX - 128 * (TILES - 1)
-    edge = jnp.pad(frames[0, :, :, PIX - last :].reshape(rows * STACK, last), ((0, 0), (0, 128 - last)))
+    facts = [
+        v.reshape(1, rows) for v in (taken_actions, next_actions, rewards, discounts, importance, buffer_slots)
+    ]
+    edge = frames[0, :, :, 128 * (TILES - 1) :]
     weights = (
         conv1_weight[0].T, conv2_weight[0].T, conv3_weight[0].T, dense_weight[0],
         conv1_bias, conv2_bias, conv3_bias, dense_bias, head_weight[0].T, head_bias,
     )
-    wide_frames, dense, sums = core(plan, frames, edge, weights, cols, (lane_action, compact))
-    frame_part, w4, k1, b1, k2, b2, k3, b3, b4, w5, b5, losses = finish(plan, wide_frames, dense, sums)
-    own = slots // (roles * batch)
-    priorities = lax.dynamic_slice_in_dim(losses.reshape(-1), (role * batch + place) * own, own, 0)
-    return (frame_part, k1.T, b1[0], k2.T, b2[0], k3.T, b3[0], w4, b4[0], w5.T, b5[0], priorities)
+    partial = core(plan, frames, edge, weights, facts, (lane_action, compact))
+    frame_part, w4, k1, b1, k2, b2, k3, b3, b4, w5, b5, priorities = finish(plan, slots // (roles * batch), *partial)
+    return (frame_part, k1.T, b1[0], k2.T, b2[0], k3.T, b3[0], w4, b4[0], w5.T, b5[0], priorities[0])
 
 
 def solution(mesh):

time: 206 us -> 183 us (0.89)
  Pallas kernels: 196 us -> 178 us
  local copies, waits for them, and re-layouts: 7.19 us -> 1.82 us
    pallas_call x1, Pallas kernels: 182 us -> 164 us  [core(): pl.pallas_call(functools.partial(core_kernel, plan, steps), in_specs=[hbm...]
    unnamed x5 -> x0, local copies, waits for them, and re-layouts: 3.2 us -> none
where the time goes in v2:
time: 183 us; the launch traced here: 180 us
  Pallas kernels  178 us (97%)
    pallas_call x1, Pallas kernels, core(): pl.pallas_call(functools.partial(core_kernel, plan, steps), in_specs=[hbm...  164 us
    pallas_call x1, Pallas kernels, finish(): pl.pallas_call(functools.partial(finish_kernel, plan, own), grid=(rows //...  13.6 us

profile of v2, /device:TPU:14, one launch (start us, length us, event | category | flops | bytes accessed | tf_op | source)
XLA Modules:
  0.0 180.2 jit_solution(14303517704999662745)
XLA Ops:
  0.6 1.8 %slice_bitcast_fusion.refs_1_ = f32[224,4,16]{2,1,0:T(4,128)} fusion(f32[1,224,4,7056]{3,2,1,0:T(4,128)} %refs_0_.1), kind=kLoop, calls=%fused_computation | loop fusion | bytes 114688 | tf_op jit(solution)/shard_map/squeeze | solution.py:1017
  2.5 163.9 %core.1 = (f32[224,2,7168]{2,1,0:T(2,128)}, bf16[3136,512]{1,0:T(8,128)(2,1)}, bf16[1216,512]{1,0:T(8,128)(2,1)}, bf16[6,21,32,1536]{3,2,1,0:T(8,128)(2,1)}, bf1...) custom-call(f32[1,224,4,7056]{3,2,1,0:T(4,128)} %refs_0_.1, ...), custom_call_target="tpu_custom_call" | custom-call | tf_op jit(solution)/shard_map/core/pallas_call | solution.py:915
  166.4 13.6 %finish.1 = (f32[224,2,7056]{2,1,0:T(2,128)}, f32[3136,512]{1,0:T(8,128)}, f32[32,256]{1,0:T(8,128)}, f32[1,32]{1,0:T(1,128)}, f32[64,512]{1,0:T(8,128)}, /*inde...) custom-call(f32[224,2,7168]{2,1,0:T(2,128)} %get-tuple-element.27.fr, ...), custom_call_target="tpu_custom_call" | custom-call | tf_op jit(solution)/shard_map/finish/pallas_call | solution.py:969

commit v3 on v2

--- a/solution.py
+++ b/solution.py
@@ -261,13 +261,11 @@
                 w4[64 * spot : 64 * spot + 64, low : low + 128] = spare[
                     1, pl.ds(3136 * q + spot, 64, stride=49), :
                 ].astype(BF16)
-    total_step(1)
     build_picks(send)
     bias[...] = jnp.zeros_like(bias)
     for at, (ref, size, copies) in enumerate(((b1_ref, 32, 20), (b2_ref, 64, 9), (b3_ref, 64, 7))):
         repeat = onehot((iota((size, size * copies), 1) & (size - 1)) == iota((size, size * copies), 0), F32)
         bias[at : at + 1, : size * copies] = dot(ref[...], repeat, precision=HIGHEST)
-    total_step(2)
     acc1[...] = jnp.zeros_like(acc1)
     acc2[...] = jnp.zeros_like(acc2)
     acc3[...] = jnp.zeros_like(acc3)
@@ -455,12 +453,12 @@
             for c in keep_copies(step, 0, 3):
                 c.start()
 
+    total_step(1)
     raw_wait(0, 0)
     prefetch(1, 1)
-    hooks = [functools.partial(total_step, stage) for stage in range(3, plan.bits + 1)]
-    slope4[...] = forward(0, 0, hooks[:6])
-    for late in hooks[6:]:
-        late()
+    slope4[...] = forward(0, 0, [functools.partial(total_step, 2), lambda: None, functools.partial(total_step, 3)])
+    for stage in range(4, plan.bits + 1):
+        total_step(stage)
     after_forward(0)
 
     def one_step(step, _):
@@ -657,12 +655,11 @@
             keep = aligned(low + bit_of(order[stage]) * half)
             into = base + size - count
             target = final if stage == plan.bits - 1 else send
-            block = 64 if half % 64 == 0 else 16
+            block = next(b for b in (128, 64, 32, 16) if half % b == 0)
 
             def add(i, _, keep=keep, into=into, target=target, block=block):
                 at = aligned(keep + i * block)
-                new = landed[pl.ds(aligned(into + i * block), block)].astype(F32)
-                target[pl.ds(at, block)] = (send[pl.ds(at, block)].astype(F32) + new).astype(BF16)
+                target[pl.ds(at, block)] = send[pl.ds(at, block)] + landed[pl.ds(aligned(into + i * block), block)]
                 return 0
 
             lax.fori_loop(0, half // block, add, 0)
@@ -728,7 +725,7 @@
     bits, first, second = plan.bits, plan.first, plan.second
 
     late_grads = [(step, half) for step in range(early, steps) for half in range(2)]
-    issue = {"soon": late_grads[:-4], "mid": late_grads[-4:-3], "over": late_grads[-3:-2], "last": late_grads[-2:]}
+    issue = {"soon": late_grads[:-4], "mid": late_grads[-4:-2], "over": late_grads[-2:-1], "last": late_grads[-1:]}
 
     def grads_at(moment):
         for step, half in issue[moment]:
@@ -745,7 +742,7 @@
         def turns(turn, _):
             weight_step(turn, jnp.where(turn == 0, steps - 1, turn - 1))
 
-            @pl.when(turn == turn_at(1))
+            @pl.when(turn == 0)
             def _():
                 scatter_finish(0, first)
                 grads_at("soon")
@@ -775,10 +772,10 @@
         @pl.when(online & (step == 0))
         def _():
             scatter_finish(0, second)
+
+        @pl.when(online & (step == turn_at(1)))
+        def _():
             scatter_finish(2, first)
-
-        @pl.when(online & (step == turn_at(1)))
-        def _():
             scatter_finish(1, second)
 
         @pl.when(online & (step == turn_at(2)))
@@ -793,21 +790,30 @@
             for stage in range(3, bits):
                 scatter_finish(stage, second)
             grads_at("last")
-
-        @pl.when(online & (step == turn_at(5)))
-        def _():
             gather_finish(0, first)
+
+        @pl.when(online & (step == turn_at(4)))
+        def _():
             gather_finish(0, second)
 
         @pl.when((role == 1) & (step == max(steps - 3, 0)))
         def _():
             over_finish(first)
-            for stage in range(bits):
+            gather_finish(0, first)
+            over_finish(second)
+            for stage in range(1, bits - 2):
                 gather_finish(stage, first)
-                if stage == 0:
-                    over_finish(second)
-                else:
-                    gather_finish(stage - 1, second)
+                gather_finish(stage - 1, second)
+
+        @pl.when((role == 1) & (step == max(steps - 2, 0)))
+        def _():
+            gather_finish(bits - 2, first)
+            gather_finish(bits - 3, second)
+            gather_finish(bits - 2, second)
+
+        @pl.when((role == 1) & (step == steps - 1))
+        def _():
+            gather_finish(bits - 1, first)
             gather_finish(bits - 1, second)
 
         return 0

time: 183 us -> 186 us (1.016)
  Pallas kernels: 178 us -> 182 us
    pallas_call x1, Pallas kernels: 164 us -> 168 us  [core(): pl.pallas_call(functools.partial(core_kernel, plan, steps), in_specs=[hbm...]
where the time goes in v3:
time: 186 us; the launch traced here: 185 us
  Pallas kernels  182 us (98%)
    pallas_call x1, Pallas kernels, core(): pl.pallas_call(functools.partial(core_kernel, plan, steps), in_specs=[hbm...  168 us
    pallas_call x1, Pallas kernels, finish(): pl.pallas_call(functools.partial(finish_kernel, plan, own), grid=(rows //...  13.6 us

profile of v3, /device:TPU:14, one launch (start us, length us, event | category | flops | bytes accessed | tf_op | source)
XLA Modules:
  0.0 184.6 jit_solution(9627576829375773641)
XLA Ops:
  0.6 1.8 slice_bitcast_fusion.refs_1_
  2.5 168.4 %core.1 = (f32[224,2,7168]{2,1,0:T(2,128)}, bf16[3136,512]{1,0:T(8,128)(2,1)}, bf16[1216,512]{1,0:T(8,128)(2,1)}, bf16[6,21,32,1536]{3,2,1,0:T(8,128)(2,1)}, bf1...) custom-call(f32[1,224,4,7056]{3,2,1,0:T(4,128)} %refs_0_.1, ...), custom_call_target="tpu_custom_call" | custom-call | tf_op jit(solution)/shard_map/core/pallas_call | solution.py:921
  170.8 13.6 %finish.1 = (f32[224,2,7056]{2,1,0:T(2,128)}, f32[3136,512]{1,0:T(8,128)}, f32[32,256]{1,0:T(8,128)}, f32[1,32]{1,0:T(1,128)}, f32[64,512]{1,0:T(8,128)}, /*inde...) custom-call(f32[224,2,7168]{2,1,0:T(2,128)} %get-tuple-element.27.fr, ...), custom_call_target="tpu_custom_call" | custom-call | tf_op jit(solution)/shard_map/finish/pallas_call | solution.py:975

commit v4 on v3

--- a/solution.py
+++ b/solution.py
@@ -725,7 +725,7 @@
     bits, first, second = plan.bits, plan.first, plan.second
 
     late_grads = [(step, half) for step in range(early, steps) for half in range(2)]
-    issue = {"soon": late_grads[:-4], "mid": late_grads[-4:-2], "over": late_grads[-2:-1], "last": late_grads[-1:]}
+    issue = {"soon": late_grads[:-4], "mid": late_grads[-4:-3], "over": late_grads[-3:-2], "last": late_grads[-2:]}
 
     def grads_at(moment):
         for step, half in issue[moment]:
@@ -742,7 +742,7 @@
         def turns(turn, _):
             weight_step(turn, jnp.where(turn == 0, steps - 1, turn - 1))
 
-            @pl.when(turn == 0)
+            @pl.when(turn == turn_at(1))
             def _():
                 scatter_finish(0, first)
                 grads_at("soon")
@@ -772,10 +772,10 @@
         @pl.when(online & (step == 0))
         def _():
             scatter_finish(0, second)
+            scatter_finish(2, first)
 
         @pl.when(online & (step == turn_at(1)))
         def _():
-            scatter_finish(2, first)
             scatter_finish(1, second)
 
         @pl.when(online & (step == turn_at(2)))
@@ -790,10 +790,10 @@
             for stage in range(3, bits):
                 scatter_finish(stage, second)
             grads_at("last")
+
+        @pl.when(online & (step == turn_at(5)))
+        def _():
             gather_finish(0, first)
-
-        @pl.when(online & (step == turn_at(4)))
-        def _():
             gather_finish(0, second)
 
         @pl.when((role == 1) & (step == max(steps - 3, 0)))

time: 186 us -> 179 us (0.962); the launches traced: 185 us -> 176 us
  Pallas kernels: 182 us -> 173 us
    pallas_call x1, Pallas kernels: 168 us -> 159 us  [core(): pl.pallas_call(functools.partial(core_kernel, plan, steps), in_specs=[hbm...]
where the time goes in v4:
time: 179 us; the launch traced here: 176 us
  Pallas kernels  173 us (97%)
  local copies, waits for them, and re-layouts  1.82 us (1%)
    pallas_call x1, Pallas kernels, core(): pl.pallas_call(functools.partial(core_kernel, plan, steps), in_specs=[hbm...  159 us
    pallas_call x1, Pallas kernels, finish(): pl.pallas_call(functools.partial(finish_kernel, plan, own), grid=(rows //...  13.6 us

profile of v4, /device:TPU:14, one launch (start us, length us, event | category | flops | bytes accessed | tf_op | source)
XLA Modules:
  0.0 175.7 jit_solution(13293058450301291728)
XLA Ops:
  0.6 1.8 %slice_bitcast_fusion.refs_1_ = f32[224,4,16]{2,1,0:T(4,128)} fusion(f32[1,224,4,7056]{3,2,1,0:T(4,128)} %refs_0_.1), kind=kLoop, calls=%fused_computation | loop fusion | bytes 114688 | tf_op jit(solution)/shard_map/squeeze | solution.py:1023
  2.5 159.4 %core.1 = (f32[224,2,7168]{2,1,0:T(2,128)}, bf16[3136,512]{1,0:T(8,128)(2,1)}, bf16[1216,512]{1,0:T(8,128)(2,1)}, bf16[6,21,32,1536]{3,2,1,0:T(8,128)(2,1)}, bf1...) custom-call(f32[1,224,4,7056]{3,2,1,0:T(4,128)} %refs_0_.1, ...), custom_call_target="tpu_custom_call" | custom-call | tf_op jit(solution)/shard_map/core/pallas_call | solution.py:921
  161.9 13.6 %finish.1 = (f32[224,2,7056]{2,1,0:T(2,128)}, f32[3136,512]{1,0:T(8,128)}, f32[32,256]{1,0:T(8,128)}, f32[1,32]{1,0:T(1,128)}, f32[64,512]{1,0:T(8,128)}, /*inde...) custom-call(f32[224,2,7168]{2,1,0:T(2,128)} %get-tuple-element.27.fr, ...), custom_call_target="tpu_custom_call" | custom-call | tf_op jit(solution)/shard_map/finish/pallas_call | solution.py:975

commit v5 on v4

--- a/solution.py
+++ b/solution.py
@@ -291,11 +291,12 @@
         own = cols[rows, :]
         for kind in range(8):
             bands = list(range(kind, 21, 8))
+            width = 384 if (BAND * kind) % 128 + BAND <= 384 else 512
             for at, band in enumerate(bands):
                 low = BAND * band // 128
                 for c in range(STACK):
                     place_at = (at * STACK + c) * SUB
-                    for t in range(4):
+                    for t in range(width // 128):
                         if low + t < TILES - 1:
                             piece = raw_flat[slot, low + t, pl.ds(c, SUB, stride=STACK), :]
                         else:
@@ -303,7 +304,7 @@
                             piece = jnp.concatenate([piece, jnp.zeros((SUB, 128 - piece.shape[1]), F32)], axis=1)
                         lines[place_at : place_at + SUB, 128 * t : 128 * t + 128] = piece.astype(BF16)
             count = len(bands) * STACK * SUB
-            sorted_lines = dot(lines[:count], send[512 * kind : 512 * kind + 512, :WIDE]).astype(BF16)
+            sorted_lines = dot(lines[:count, :width], send[512 * kind : 512 * kind + width, :WIDE]).astype(BF16)
             for at, band in enumerate(bands):
                 for c in range(STACK):
                     place_at = (at * STACK + c) * SUB
@@ -683,6 +684,18 @@
             final.at[spot], final.at[spot], ag_send.at[index], ag_recv.at[index], across(order[plan.bits - 1 - stage])
         )
 
+    def result_copies(stream):
+        low, size, _ = plan.streams[stream]
+        cut = min(max(low, ROW_HEAD), low + size)
+        found = []
+        if low < cut:
+            spot = pl.ds(low, cut - low)
+            found.append(pltpu.make_async_copy(final.at[spot], dense_out.at[spot], out_sem.at[2 * stream]))
+        if cut < low + size:
+            here, there = pl.ds(cut, low + size - cut), pl.ds(cut - ROW_HEAD, low + size - cut)
+            found.append(pltpu.make_async_copy(final.at[here], sums_out.at[there], out_sem.at[2 * stream + 1]))
+        return found
+
     def over_finish(streams):
         for stream in streams:
             over_copy(stream).wait_recv()
@@ -693,6 +706,9 @@
             gather_copy(stream, stage).wait_recv()
             if stage + 1 < plan.bits:
                 gather_copy(stream, stage + 1).start()
+            else:
+                for c in result_copies(stream):
+                    c.start()
 
     tile_rows = raw.reshape(2 * (TILES - 1) * SUB * STACK, 128)
 
@@ -826,13 +842,6 @@
             gather_finish(stage, first)
             gather_finish(stage, second)
 
-    out_copies = [
-        pltpu.make_async_copy(final.at[pl.ds(0, ROW_HEAD)], dense_out, out_sem.at[0]),
-        pltpu.make_async_copy(final.at[pl.ds(ROW_HEAD, plan.rows - ROW_HEAD)], sums_out, out_sem.at[1]),
-    ]
-    for c in out_copies:
-        c.start()
-
     for c in tile_copies(steps - 1):
         c.wait()
     for stream in range(len(plan.streams)):
@@ -862,8 +871,9 @@
 
         lax.fori_loop(0, steps, sent, 0)
 
-    for c in out_copies:
-        c.wait()
+    for stream in range(len(plan.streams)):
+        for c in result_copies(stream):
+            c.wait()
 
 
 def core(plan, frames, edge, weights, facts, tables):
@@ -916,7 +926,7 @@
         dma((5,)), dma((5,)), dma((2,)), dma, dma, dma((steps,)), dma((steps,)), dma((2 * steps,)), dma((2 * steps,)),
         dma((plan.bits,)), dma((plan.bits,)), dma, dma,
         dma((streams * plan.bits,)), dma((streams * plan.bits,)), dma((streams * plan.bits,)), dma((streams * plan.bits,)),
-        dma((streams,)), dma((streams,)), dma((2,)),
+        dma((streams,)), dma((streams,)), dma((2 * streams,)),
     ]
     return pl.pallas_call(
         functools.partial(core_kernel, plan, steps),

time: 179 us -> 179 us (level)
  no operation moved by 1% of the time
where the time goes in v5:
time: 179 us; the launch traced here: 176 us
  Pallas kernels  173 us (97%)
  local copies, waits for them, and re-layouts  1.82 us (1%)
    pallas_call x1, Pallas kernels, core(): pl.pallas_call(functools.partial(core_kernel, plan, steps), in_specs=[hbm...  160 us
    pallas_call x1, Pallas kernels, finish(): pl.pallas_call(functools.partial(finish_kernel, plan, own), grid=(rows //...  13.6 us

profile of v5, /device:TPU:14, one launch (start us, length us, event | category | flops | bytes accessed | tf_op | source)
XLA Modules:
  0.0 175.9 jit_solution(1532127704597569391)
XLA Ops:
  0.6 1.8 %slice_bitcast_fusion.refs_1_ = f32[224,4,16]{2,1,0:T(4,128)} fusion(f32[1,224,4,7056]{3,2,1,0:T(4,128)} %refs_0_.1), kind=kLoop, calls=%fused_computation | loop fusion | bytes 114688 | tf_op jit(solution)/shard_map/squeeze | solution.py:1033
  2.5 159.6 %core.1 = (f32[224,2,7168]{2,1,0:T(2,128)}, bf16[3136,512]{1,0:T(8,128)(2,1)}, bf16[1216,512]{1,0:T(8,128)(2,1)}, bf16[6,21,32,1536]{3,2,1,0:T(8,128)(2,1)}, bf1...) custom-call(f32[1,224,4,7056]{3,2,1,0:T(4,128)} %refs_0_.1, ...), custom_call_target="tpu_custom_call" | custom-call | tf_op jit(solution)/shard_map/core/pallas_call | solution.py:931
  162.1 13.6 %finish.1 = (f32[224,2,7056]{2,1,0:T(2,128)}, f32[3136,512]{1,0:T(8,128)}, f32[32,256]{1,0:T(8,128)}, f32[1,32]{1,0:T(1,128)}, f32[64,512]{1,0:T(8,128)}, /*inde...) custom-call(f32[224,2,7168]{2,1,0:T(2,128)} %get-tuple-element.27.fr, ...), custom_call_target="tpu_custom_call" | custom-call | tf_op jit(solution)/shard_map/finish/pallas_call | solution.py:985

commit v6 on v4

--- a/solution.py
+++ b/solution.py
@@ -742,7 +742,7 @@
         def turns(turn, _):
             weight_step(turn, jnp.where(turn == 0, steps - 1, turn - 1))
 
-            @pl.when(turn == turn_at(1))
+            @pl.when(turn == 0)
             def _():
                 scatter_finish(0, first)
                 grads_at("soon")
@@ -790,10 +790,10 @@
             for stage in range(3, bits):
                 scatter_finish(stage, second)
             grads_at("last")
+            gather_finish(0, first)
 
         @pl.when(online & (step == turn_at(5)))
         def _():
-            gather_finish(0, first)
             gather_finish(0, second)
 
         @pl.when((role == 1) & (step == max(steps - 3, 0)))

time: 179 us -> 183 us (1.022); the launches traced: 176 us -> 183 us
  Pallas kernels: 173 us -> 180 us
    pallas_call x1, Pallas kernels: 159 us -> 167 us  [core(): pl.pallas_call(functools.partial(core_kernel, plan, steps), in_specs=[hbm...]
where the time goes in v6:
time: 183 us
  Pallas kernels  180 us (98%)
    pallas_call x1, Pallas kernels, core(): pl.pallas_call(functools.partial(core_kernel, plan, steps), in_specs=[hbm...  167 us
    pallas_call x1, Pallas kernels, finish(): pl.pallas_call(functools.partial(finish_kernel, plan, own), grid=(rows //...  13.6 us

profile of v6, /device:TPU:14, one launch (start us, length us, event | category | flops | bytes accessed | tf_op | source)
XLA Modules:
  0.0 183.0 jit_solution(854709855080499317)
XLA Ops:
  0.6 1.8 slice_bitcast_fusion.refs_1_
  2.5 166.7 %core.1 = (f32[224,2,7168]{2,1,0:T(2,128)}, bf16[3136,512]{1,0:T(8,128)(2,1)}, bf16[1216,512]{1,0:T(8,128)(2,1)}, bf16[6,21,32,1536]{3,2,1,0:T(8,128)(2,1)}, bf1...) custom-call(f32[1,224,4,7056]{3,2,1,0:T(4,128)} %refs_0_.1, ...), custom_call_target="tpu_custom_call" | custom-call | tf_op jit(solution)/shard_map/core/pallas_call | solution.py:921
  169.2 13.6 %finish.1 = (f32[224,2,7056]{2,1,0:T(2,128)}, f32[3136,512]{1,0:T(8,128)}, f32[32,256]{1,0:T(8,128)}, f32[1,32]{1,0:T(1,128)}, f32[64,512]{1,0:T(8,128)}, /*inde...) custom-call(f32[224,2,7168]{2,1,0:T(2,128)} %get-tuple-element.27.fr, ...), custom_call_target="tpu_custom_call" | custom-call | tf_op jit(solution)/shard_map/finish/pallas_call | solution.py:975
